TPU v7x, 256 devices: a whole 4x4x8 slice. The times are simulated.
256 devices in a mesh: section: 8 (over y, z_hi), tensor: 32 (over z_lo, x, core).
Axes of the slice: x: 4, y: 4, z: 8 (z_hi: 2, z_lo: 4; z = z_hi * 4 + z_lo), core: 2. Of those that a mesh axis runs over, the one named last changes fastest.
Arguments:
- acts: bfloat16 [8, 4096, 8192], P('section', 'tensor'), may hold values from -6 to 6
- grad_q: bfloat16 [8, 4096, 8192], P('section', 'tensor'), may hold values from -6 to 6
- grad_v: bfloat16 [8, 4096, 1024], P('section', 'tensor'), may hold values from -6 to 6
- fac_a: bfloat16 [8, 128, 131072], P('section', None, 'tensor'), may hold values from -0.0625 to 0.0625
- fac_bq: bfloat16 [8, 128, 65536], P('section', None, 'tensor'), may hold values from -0.0625 to 0.0625
- fac_bv: bfloat16 [8, 128, 8192], P('section', None, 'tensor'), may hold values from -0.1875 to 0.1875
- seq_tenant: int32 [8, 32], P('section'), may hold values from 0 to 127
- tenant_task: int32 [128], replicated, may hold values from 0 to 31
- section_layer: int32 [8], replicated, may hold values from 0 to 79
- task_emb: bfloat16 [32, 4096], replicated, may hold values from -6 to 6
- layer_emb: bfloat16 [80, 4096], replicated, may hold values from -6 to 6
Outputs:
- grad_a: bfloat16 [4096, 131072], P(None, ('tensor', 'section'))
- grad_bq: bfloat16 [4096, 65536], P(None, ('tensor', 'section'))
- grad_bv: bfloat16 [4096, 8192], P('section', 'tensor')
All inputs are finite; a program needn't handle non-finite values.
Results may differ from a plain program's by a relative error of at most 0.0064.
Values may be sent and summed in bfloat16 or wider, within the bound.
A program may use at most 64 MiB of HBM per device.

v0:
```python
import math

import jax
import jax.numpy as jnp
from jax import lax
from jax.sharding import PartitionSpec as P

D = 8192
DQ = 8192
DV = 1024
H = 4096
R = 8
TENANTS = 128


def shards(
    acts,
    grad_q,
    grad_v,
    fac_a,
    fac_bq,
    fac_bv,
    seq_tenant,
    tenant_task,
    section_layer,
    task_emb,
    layer_emb,
):
    tensor_count = lax.axis_size("tensor")
    section_count = lax.axis_size("section")
    tok_rows = acts.shape[1]
    gradient_scale_factor = 2.0 / math.sqrt(tok_rows * tensor_count * section_count)
    highest_precision_mode = lax.Precision.HIGHEST
    owners = seq_tenant[0]
    input_arrays = acts[0]
    cotan_query = grad_q[0]
    cotan_value = grad_v[0]
    full_a, full_bq, full_bv = (
        lax.all_to_all(fac_a[0][owners], "tensor", split_axis=0, concat_axis=1, tiled=True),
        lax.all_to_all(fac_bq[0][owners], "tensor", split_axis=0, concat_axis=1, tiled=True),
        lax.all_to_all(fac_bv[0][owners], "tensor", split_axis=0, concat_axis=1, tiled=True),
    )
    down_mat = full_a.reshape(D, 2 * R)
    upq_mat = full_bq.reshape(DQ, R)
    upv_mat = full_bv.reshape(DV, R)
    down_projection_weight = jnp.dot(input_arrays, down_mat, preferred_element_type=jnp.float32)
    back_query = jnp.dot(cotan_query, upq_mat, preferred_element_type=jnp.float32)
    back_value = jnp.dot(cotan_value, upv_mat, preferred_element_type=jnp.float32)
    down_round = down_projection_weight.astype(jnp.bfloat16)
    backward_rounded = jnp.concatenate([back_query, back_value], axis=-1).astype(jnp.bfloat16)
    own_a = gradient_scale_factor * jnp.einsum(
        "ld,lj->dj", input_arrays, backward_rounded, preferred_element_type=jnp.float32
    )
    own_bq = gradient_scale_factor * jnp.einsum(
        "le,lr->er", cotan_query, down_round[:, :R], preferred_element_type=jnp.float32
    )
    own_bv = gradient_scale_factor * jnp.einsum(
        "le,lr->er", cotan_value, down_round[:, R:], preferred_element_type=jnp.float32
    )
    sequence_down_factor, seq_bq, seq_bv = (
        lax.all_to_all(
            own_a.reshape(1, -1).astype(jnp.bfloat16),
            "tensor",
            split_axis=1,
            concat_axis=0,
            tiled=True,
        ),
        lax.all_to_all(
            own_bq.reshape(1, -1).astype(jnp.bfloat16),
            "tensor",
            split_axis=1,
            concat_axis=0,
            tiled=True,
        ),
        lax.all_to_all(
            own_bv.reshape(1, -1).astype(jnp.bfloat16),
            "tensor",
            split_axis=1,
            concat_axis=0,
            tiled=True,
        ),
    )
    all_owners = lax.all_gather(seq_tenant, "section", axis=0, tiled=True)
    task_rows = task_emb[tenant_task].astype(jnp.float32)
    layer_rows = layer_emb[section_layer].astype(jnp.float32)
    head_seq = (
        jax.nn.silu(layer_rows[:, None, :] + task_rows[all_owners])
        .astype(jnp.bfloat16)
        .reshape(-1, H)
    )
    tenant_ids = jnp.arange(TENANTS, dtype=jnp.int32)
    onehot = (tenant_ids[:, None] == owners[None, :]).astype(jnp.float32)
    ten_a = jnp.dot(
        onehot, sequence_down_factor.astype(jnp.float32), precision=highest_precision_mode
    )
    ten_bq = jnp.dot(onehot, seq_bq.astype(jnp.float32), precision=highest_precision_mode)
    column_a, column_bq = (
        lax.all_to_all(ten_a, "section", split_axis=1, concat_axis=0, tiled=True),
        lax.all_to_all(ten_bq, "section", split_axis=1, concat_axis=0, tiled=True),
    )
    head_in = (
        jax.nn.silu(layer_rows[:, None, :] + task_rows[None, :, :])
        .astype(jnp.bfloat16)
        .reshape(-1, H)
        .astype(jnp.float32)
    )
    grad_a = jnp.einsum(
        "ph,pc->hc",
        head_in,
        column_a,
        precision=highest_precision_mode,
        preferred_element_type=jnp.float32,
    ).astype(jnp.bfloat16)
    grad_bq = jnp.einsum(
        "ph,pc->hc",
        head_in,
        column_bq,
        precision=highest_precision_mode,
        preferred_element_type=jnp.float32,
    ).astype(jnp.bfloat16)
    every_bv = lax.all_gather(seq_bv, "section", axis=0, tiled=True)
    row_share = H // section_count
    own_rows = lax.dynamic_slice_in_dim(
        head_seq, lax.axis_index("section") * row_share, row_share, 1
    )
    grad_bv = jnp.einsum(
        "ph,pc->hc", own_rows, every_bv, preferred_element_type=jnp.float32
    ).astype(jnp.bfloat16)
    return (grad_a, grad_bq, grad_bv)


def solution(mesh):
    placed = (
        P("section", "tensor", None),
        P("section", "tensor", None),
        P("section", "tensor", None),
        P("section", None, "tensor"),
        P("section", None, "tensor"),
        P("section", None, "tensor"),
        P("section", None),
        P(),
        P(),
        P(),
        P(),
    )
    return jax.shard_map(
        shards,
        mesh=mesh,
        in_specs=placed,
        out_specs=(
            P(None, ("tensor", "section")),
            P(None, ("tensor", "section")),
            P("section", "tensor"),
        ),
        check_vma=False,
    )
```

profile of v0, /device:TPU:66, one launch (start us, length us, event | category | flops | bytes accessed | tf_op | source)
XLA Modules:
  0.0 288.4 jit_solution(17446001990381607553)
XLA Ops:
  0.7 0.8 fusion.62
  1.5 1.5 gather_fusion.3
  3.0 0.5 broadcast.70
  3.5 0.6 reduce.3
  4.1 0.6 reshape.210
  4.7 8.1 %all-to-all-start.1 = ((bf16[32,2,128]{2,1,0:T(2,128)(2,1)}), bf16[32,2,128]{2,1,0:T(2,128)(2,1)S(1)}, u32[]{:S(2)}, u32[]{:S(2)}) async-start(bf16[32,2,128]{2,1,0:T(2,128)(2,1)} %reshape.210), calls=%async_computation.1 | async-start | bytes 32768 | tf_op jit(solution)/shard_map/all_to_all | solution.py:41
  12.8 1.9 gather_fusion.2
  14.7 0.6 reduce.4
  15.3 0.7 reshape.212
  16.1 1.4 all-to-all-done.1
  17.5 6.9 %all-to-all-start = ((bf16[32,2,1024]{2,1,0:T(2,128)(2,1)}), bf16[32,2,1024]{2,1,0:T(2,128)(2,1)S(1)}, u32[]{:S(2)}, u32[]{:S(2)}) async-start(bf16[32,2,1024]{2,1,0:T(2,128)(2,1)} %reshape.212), calls=%async_computation | async-start | bytes 262144 | tf_op jit(solution)/shard_map/all_to_all | solution.py:40
  24.4 0.8 gather_fusion.4
  25.2 0.7 reduce.6
  25.9 0.9 reshape.216
  26.8 0.1 reduce.1
  26.9 0.3 reshape.147
  27.2 2.9 all-to-all-done
  30.1 6.8 %all-to-all-start.4 = ((bf16[32,2,2048]{2,1,0:T(2,128)(2,1)}), bf16[32,2,2048]{2,1,0:T(2,128)(2,1)S(1)}, u32[]{:S(2)}, u32[]{:S(2)}) async-start(bf16[32,2,2048]{2,1,0:T(2,128)(2,1)} %reshape.216), calls=%async_computation.4 | async-start | bytes 524288 | tf_op jit(solution)/shard_map/all_to_all | solution.py:39
  36.9 1.2 fusion.38
  38.1 0.1 reshape.213
  38.2 0.7 reduce
  39.0 3.4 %reshape.146 = bf16[8192,8]{1,0:T(8,128)(2,1)} reshape(bf16[32,2048]{1,0:T(8,128)(2,1)S(1)} %reduce) | data formatting | bytes 262144 | tf_op jit(solution)/shard_map/reshape | solution.py:44
  42.4 3.1 %fusion.39 = bf16[128,8]{0,1:T(8,128)(2,1)S(1)} fusion(bf16[8192,8]{1,0:T(8,128)(2,1)} %reshape.146, bf16[1,128,8192]{2,1,0:T(8,128)(2,1)} %param.12), kind=kOutput, calls=%fused_computation.40 | convolution fusion | flops 16778240 | bytes 2230272 | tf_op jit(solution)/shard_map/dot_general | solution.py:47
  45.5 0.3 reshape.217
  45.8 1.5 reduce.2
  47.4 2.7 reshape.148
  50.0 2.3 fusion.32
  52.3 0.2 fusion.28
  52.5 0.2 copy.39
  52.7 0.3 convert_element_type.115
  52.9 0.6 reduce.8
  53.6 0.6 reshape.220
  54.2 7.7 %all-to-all-start.7 = ((bf16[32,2,128]{2,1,0:T(2,128)(2,1)}), bf16[32,2,128]{2,1,0:T(2,128)(2,1)S(1)}, u32[]{:S(2)}, u32[]{:S(2)}) async-start(bf16[32,2,128]{2,1,0:T(2,128)(2,1)} %reshape.220), calls=%async_computation.7 | async-start | bytes 32768 | tf_op jit(solution)/shard_map/all_to_all | solution.py:75
  62.0 2.0 fusion.7
  63.9 1.7 copy.36
  65.6 3.8 %convert_element_type.114 = bf16[1,32,2048]{2,0,1:T(2,128)(2,1)S(1)} reshape(bf16[8192,8]{1,0:T(8,128)(2,1)} %copy.36) | data formatting | bytes 262144 | tf_op jit(solution)/shard_map/convert_element_type | solution.py:69
  69.5 1.3 reduce.7
  70.8 0.7 reshape.218
  71.5 7.7 %all-to-all-start.5 = ((bf16[32,2,1024]{2,1,0:T(2,128)(2,1)}), bf16[32,2,1024]{2,1,0:T(2,128)(2,1)S(1)}, u32[]{:S(2)}, u32[]{:S(2)}) async-start(bf16[32,2,1024]{2,1,0:T(2,128)(2,1)} %reshape.218), calls=%async_computation.5 | async-start | bytes 262144 | tf_op jit(solution)/shard_map/all_to_all | solution.py:68
  79.2 0.4 fusion.5
  79.6 1.7 copy.32
  81.3 3.3 %convert_element_type.113 = bf16[1,32,4096]{2,0,1:T(2,128)(2,1)S(1)} reshape(bf16[8192,16]{1,0:T(8,128)(2,1)} %copy.32) | data formatting | bytes 524288 | tf_op jit(solution)/shard_map/convert_element_type | solution.py:62
  84.7 2.1 reduce.5
  86.8 0.9 reshape.214
  87.6 7.7 %all-to-all-start.2 = ((bf16[32,2,2048]{2,1,0:T(2,128)(2,1)}), bf16[32,2,2048]{2,1,0:T(2,128)(2,1)S(1)}, u32[]{:S(2)}, u32[]{:S(2)}) async-start(bf16[32,2,2048]{2,1,0:T(2,128)(2,1)} %reshape.214), calls=%async_computation.2 | async-start | bytes 524288 | tf_op jit(solution)/shard_map/all_to_all | solution.py:61
  95.4 0.1 reshape.219
  95.6 1.4 fusion.48
  97.0 6.8 %all-to-all-done.2 = bf16[32,2,2048]{2,1,0:T(2,128)(2,1)S(1)} async-done(((bf16[32,2,2048]{2,1,0:T(2,128)(2,1)}), bf16[32,2,2048]{2,1,0:T(2,128)(2,1)S(1)}, u32[]{:S(2)}, u32[]{:S(2)}) %all-to-all-start.2) | async-done | bytes 262176 | tf_op jit(solution)/shard_map/all_to_all | solution.py:61
  103.8 8.4 %all-to-all-start.6 = ((f32[128,8,256]{2,0,1:T(8,128)}), f32[128,8,256]{2,0,1:T(8,128)}, u32[]{:S(2)}, u32[]{:S(2)}) async-start(f32[128,8,256]{2,0,1:T(8,128)} %fusion.48), calls=%async_computation.6 | async-start | bytes 2097152 | tf_op jit(solution)/shard_map/all_to_all | solution.py:99
  112.3 1.2 gather_fusion.1
  113.5 1.6 copy.29
  115.1 1.5 convert_element_type.96
  116.6 1.8 gather_fusion
  118.5 37.8 %all-gather.1 = s32[8,1,32]{2,1,0:T(1,128)S(1)} all-gather(s32[1,1,32]{2,1,0:T(1,128)S(1)} %bitcast.110), channel_id=1, replica_groups=mesh['section'=8,'tensor'=32] {'section'}, dimensions={0}, use_global_device_ids=true | all-gather | bytes 1152 | tf_op jit(solution)/shard_map/all_gather | solution.py:83
  156.4 7.3 %gather_fusion.5 = f32[256,4096]{1,0:T(8,128)} fusion(f32[128,4096]{1,0:T(8,128)} %convert_element_type.96, s32[1024]{0:T(1024)S(1)} %pad_clamp_fusion), kind=kCustom, calls=%fused_computation.5 | custom fusion | bytes 8389632 | tf_op jit(solution)/shard_map/gather | solution.py:87
  163.7 0.3 reshape.215
  164.0 0.3 copy.42
  164.3 1.9 fusion.43
  166.1 6.6 %all-to-all-start.3 = ((f32[128,8,512]{2,0,1:T(8,128)}), f32[128,8,512]{2,0,1:T(8,128)}, u32[]{:S(2)}, u32[]{:S(2)}) async-start(f32[128,8,512]{2,0,1:T(8,128)} %fusion.43), calls=%async_computation.3 | async-start | bytes 4194304 | tf_op jit(solution)/shard_map/all_to_all | solution.py:98
  172.7 4.7 %broadcast_add_fusion = f32[8,32,4096]{2,1,0:T(8,128)} fusion(f32[8,32,4096]{2,1,0:T(8,128)} %bitcast.92, f32[8,4096]{1,0:T(8,128)S(1)} %convert_element_type.95), kind=kLoop, calls=%fused_computation.30 | loop fusion | flops 1048576 | bytes 8519680 | tf_op jit(solution)/shard_map/add | solution.py:87
  177.5 78.5 %all-gather = bf16[1,256,256]{2,1,0:T(8,128)(2,1)S(1)} all-gather(bf16[1,32,256]{2,1,0:T(8,128)(2,1)S(1)} %copy.41), channel_id=2, replica_groups=mesh['section'=8,'tensor'=32] {'section'}, dimensions={1}, use_global_device_ids=true | all-gather | bytes 147456 | tf_op jit(solution)/shard_map/all_gather | solution.py:121
  256.0 2.1 convolution_convert_fusion
  258.1 12.0 %fusion.17 = bf16[4096,256]{1,0:T(8,128)(2,1)} fusion(f32[128,4096]{0,1:T(8,128)S(1)} %copy-done.3, f32[8,4096]{1,0:T(8,128)S(1)} %convert_element_type.95, f32[128,8,256]{2,0,1:T(8,128)} %all-to-all-done.6), kind=kOutput, calls=%fused_computation.22 | convolution fusion | flops 12911116288 | bytes 5373952 | tf_op jit(solution)/shard_map/ph,pc->hc/dot_general | solution.py:114
  270.0 18.3 %bitcast_convert_fusion = bf16[4096,512]{1,0:T(8,128)(2,1)} fusion(f32[128,4096]{0,1:T(8,128)} %copy.29, f32[8,4096]{1,0:T(8,128)S(1)} %convert_element_type.95, f32[128,8,512]{2,0,1:T(8,128)} %all-to-all-done.3), kind=kOutput, calls=%fused_computation.18 | convolution fusion | flops 25797066752 | bytes 8519680 | tf_op jit(solution)/shard_map/ph,pc->hc/dot_general | solution.py:107
  (40 shorter events, 0.3 us)
Async XLA Ops:
  0.6 49.4 %copy-start = (bf16[1,128,8192]{2,1,0:T(8,128)(2,1)S(1)}, bf16[1,128,8192]{2,1,0:T(8,128)(2,1)}, u32[]{:S(2)}) copy-start(bf16[1,128,8192]{2,1,0:T(8,128)(2,1)} %param.11) | copy-start | bytes 6291460
  0.6 23.7 %copy-start.2 = (bf16[1,128,4096]{2,1,0:T(8,128)(2,1)S(1)}, bf16[1,128,4096]{2,1,0:T(8,128)(2,1)}, u32[]{:S(2)}) copy-start(bf16[1,128,4096]{2,1,0:T(8,128)(2,1)} %param.14) | copy-start | bytes 3145732
  1.5 13.2 %copy-start.7 = (s32[1024]{0:T(1024)}, s32[1024]{0:T(1024)S(1)}, u32[]{:S(2)}) copy-start(s32[1024]{0:T(1024)S(1)} %pad_clamp_fusion.1) | copy-start | bytes 12292
  4.7 12.8 %all-to-all-start.1 = ((bf16[32,2,128]{2,1,0:T(2,128)(2,1)}), bf16[32,2,128]{2,1,0:T(2,128)(2,1)S(1)}, u32[]{:S(2)}, u32[]{:S(2)}) async-start(bf16[32,2,128]{2,1,0:T(2,128)(2,1)} %reshape.210), calls=%async_computation.1 | async-start | bytes 32768 | tf_op jit(solution)/shard_map/all_to_all | solution.py:41
  17.5 12.6 %all-to-all-start = ((bf16[32,2,1024]{2,1,0:T(2,128)(2,1)}), bf16[32,2,1024]{2,1,0:T(2,128)(2,1)S(1)}, u32[]{:S(2)}, u32[]{:S(2)}) async-start(bf16[32,2,1024]{2,1,0:T(2,128)(2,1)} %reshape.212), calls=%async_computation | async-start | bytes 262144 | tf_op jit(solution)/shard_map/all_to_all | solution.py:40
  30.1 15.4 %all-to-all-start.4 = ((bf16[32,2,2048]{2,1,0:T(2,128)(2,1)}), bf16[32,2,2048]{2,1,0:T(2,128)(2,1)S(1)}, u32[]{:S(2)}, u32[]{:S(2)}) async-start(bf16[32,2,2048]{2,1,0:T(2,128)(2,1)} %reshape.216), calls=%async_computation.4 | async-start | bytes 524288 | tf_op jit(solution)/shard_map/all_to_all | solution.py:39
  50.0 2.3 copy-start.6
  54.2 17.3 %all-to-all-start.7 = ((bf16[32,2,128]{2,1,0:T(2,128)(2,1)}), bf16[32,2,128]{2,1,0:T(2,128)(2,1)S(1)}, u32[]{:S(2)}, u32[]{:S(2)}) async-start(bf16[32,2,128]{2,1,0:T(2,128)(2,1)} %reshape.220), calls=%async_computation.7 | async-start | bytes 32768 | tf_op jit(solution)/shard_map/all_to_all | solution.py:75
  71.5 16.2 %all-to-all-start.5 = ((bf16[32,2,1024]{2,1,0:T(2,128)(2,1)}), bf16[32,2,1024]{2,1,0:T(2,128)(2,1)S(1)}, u32[]{:S(2)}, u32[]{:S(2)}) async-start(bf16[32,2,1024]{2,1,0:T(2,128)(2,1)} %reshape.218), calls=%async_computation.5 | async-start | bytes 262144 | tf_op jit(solution)/shard_map/all_to_all | solution.py:68
  81.3 14.3 %copy-start.8 = (s32[1,32]{1,0:T(1,128)S(1)}, s32[1,32]{1,0:T(1,128)}, u32[]{:S(2)}) copy-start(s32[1,32]{1,0:T(1,128)} %param.17) | copy-start | bytes 388
  87.6 16.2 %all-to-all-start.2 = ((bf16[32,2,2048]{2,1,0:T(2,128)(2,1)}), bf16[32,2,2048]{2,1,0:T(2,128)(2,1)S(1)}, u32[]{:S(2)}, u32[]{:S(2)}) async-start(bf16[32,2,2048]{2,1,0:T(2,128)(2,1)} %reshape.214), calls=%async_computation.2 | async-start | bytes 524288 | tf_op jit(solution)/shard_map/all_to_all | solution.py:61
  95.4 16.8 %copy-start.9 = (s32[128]{0:T(128)S(1)}, s32[128]{0:T(128)}, u32[]{:S(2)}) copy-start(s32[128]{0:T(128)} %param.18) | copy-start | bytes 1540
  95.4 16.9 %copy-start.1 = (bf16[32,4096]{1,0:T(8,128)(2,1)S(1)}, bf16[32,4096]{1,0:T(8,128)(2,1)}, u32[]{:S(2)}) copy-start(bf16[32,4096]{1,0:T(8,128)(2,1)} %param.20) | copy-start | bytes 786436
  103.8 8.4 %copy-start.4 = (bf16[32,2,2048]{2,1,0:T(2,128)(2,1)}, bf16[32,2,2048]{2,1,0:T(2,128)(2,1)S(1)}, u32[]{:S(2)}) copy-start(bf16[32,2,2048]{2,1,0:T(2,128)(2,1)S(1)} %all-to-all-done.2) | copy-start | bytes 786436
  103.8 62.3 %all-to-all-start.6 = ((f32[128,8,256]{2,0,1:T(8,128)}), f32[128,8,256]{2,0,1:T(8,128)}, u32[]{:S(2)}, u32[]{:S(2)}) async-start(f32[128,8,256]{2,0,1:T(8,128)} %fusion.48), calls=%async_computation.6 | async-start | bytes 2097152 | tf_op jit(solution)/shard_map/all_to_all | solution.py:99
  115.1 1.5 copy-start.10
  156.4 7.3 %copy-start.5 = (bf16[32,2,2048]{2,1,0:T(2,128)(2,1)S(1)}, bf16[32,2,2048]{2,1,0:T(2,128)(2,1)}, u32[]{:S(2)}) copy-start(bf16[32,2,2048]{2,1,0:T(2,128)(2,1)} %copy-done.4) | copy-start | bytes 786436
  166.1 103.9 %all-to-all-start.3 = ((f32[128,8,512]{2,0,1:T(8,128)}), f32[128,8,512]{2,0,1:T(8,128)}, u32[]{:S(2)}, u32[]{:S(2)}) async-start(f32[128,8,512]{2,0,1:T(8,128)} %fusion.43), calls=%async_computation.3 | async-start | bytes 4194304 | tf_op jit(solution)/shard_map/all_to_all | solution.py:98
  177.5 80.6 %copy-start.3 = (f32[128,4096]{0,1:T(8,128)S(1)}, f32[128,4096]{0,1:T(8,128)}, u32[]{:S(2)}) copy-start(f32[128,4096]{0,1:T(8,128)} %copy.29) | copy-start | bytes 6291460
where the time goes:
time: 290 us; the launch traced here: 288 us
  blocking collectives  116 us (40%)
  starting transfers between devices  60 us (21%)
  matrix products  44.8 us (15%)
  local copies, waits for them, and re-layouts  39.9 us (14%)
  other arithmetic  15.4 us (5%)
  waiting for transfers between devices  11.1 us (4%)
    all_gather x1, blocking collectives, shards(): every_bv = lax.all_gather(seq_bv, 'section', axis=0, tiled=True)  78.5 us
    all_gather x1, blocking collectives, shards(): all_owners = lax.all_gather(seq_tenant, 'section', axis=0, tiled=True)  37.8 us
    dot_general x1, matrix products, shards(): jnp.einsum('ph,pc->hc', head_in, column_a, precision=highest_precision_mo...  18.3 us
    dot_general x1, matrix products, shards(): jnp.einsum('ph,pc->hc', head_in, column_bq, precision=highest_precision_m...  12 us
    all_to_all x1, starting transfers between devices, shards(): lax.all_to_all(ten_bq, 'section', split_axis=1, concat_axis=0, tiled=True)  8.4 us
    all_to_all x1, starting transfers between devices, shards(): lax.all_to_all(fac_bv[0][owners], 'tensor', split_axis=0, concat_axis=1,...  8.15 us
    all_to_all x1, starting transfers between devices, shards(): lax.all_to_all(own_bv.reshape(1, -1).astype(jnp.bfloat16), 'tensor', spli...  7.74 us
    all_to_all x1, starting transfers between devices, shards(): lax.all_to_all(own_a.reshape(1, -1).astype(jnp.bfloat16), 'tensor', split...  7.73 us
  transfers between devices with their start and end apart: 8, of which 3 were waited for; matrix products, arithmetic and copies ran while one was open for 24% of the time, Pallas kernels for 0%

commit v1 on v0

v1 whole, which is shorter than its diff:
```python
import functools
import math

import jax
import jax.numpy as jnp
from jax import lax
from jax.experimental import pallas as pl
from jax.experimental.pallas import tpu as pltpu
from jax.sharding import PartitionSpec as P

MESH = pl.DeviceIdType.MESH
F32, BF16 = jnp.float32, jnp.bfloat16

H = 4096
R = 8
TENANTS = 128
TASKS = 32
LAYERS = 80
TOK = 128
NS, NT = 8, 32
NX, NY, NZL, NZH, NC = 4, 4, 4, 2, 2
SCALE = 2.0 / math.sqrt(TOK * NT * NS)


def mm(a, b):
    return jnp.dot(a, b, preferred_element_type=F32)


def iota(shape, dim):
    return lax.broadcasted_iota(jnp.int32, shape, dim)


def exchange(
    acts, gq, gv, fa, fq, fv, own, task_of, layer_of, task_emb, layer_emb,
    s_a, s_q, head_out, head_own,
    acts_v, gq_v, gv_v, fa_v, fq_v, fv_v, emb_v, head_v,
    own_s, own_r, gat_a, gat_q, tr, a2, b2, v2,
    p_as, p_ar, p_qs, p_qr, z_as, z_ar, z_qs, z_qr, x_as, x_qs, big_a, big_q,
    load_sem, out_sem, own_ss, own_rs, pa_ss, pa_rs, pq_ss, pq_rs, za_ss, za_rs, zq_ss, zq_rs, xa_ss, xa_rs, xq_ss, xq_rs,
):
    s, t = lax.axis_index("section"), lax.axis_index("tensor")
    y, zh = s // 2, s % 2
    zl, x, c = t // 8, (t // 2) % 4, t % 2
    zdev = (zl * 2 + zh) * 2 + c
    xy = x * 4 + y

    loads = [
        pltpu.make_async_copy(src, dst, load_sem.at[i])
        for i, (src, dst) in enumerate(
            (
                (fq, fq_v), (fv, fv_v), (fa, fa_v), (gq, gq_v), (gv, gv_v), (acts, acts_v),
                (task_emb, emb_v.at[pl.ds(0, TASKS)]),
                (layer_emb, emb_v.at[pl.ds(TASKS, LAYERS)]),
            )
        )
    ]
    for load in loads:
        load.start()

    bar = pltpu.get_barrier_semaphore()

    def greet(section, tensor):
        pl.semaphore_signal(bar, inc=1, device_id=(section, tensor), device_id_type=MESH)

    def greet_tensor(k, _):
        greet(s, lax.rem(t + k, NT))
        return 0

    lax.fori_loop(1, NT, greet_tensor, 0)

    def greet_z(k, _):
        greet(y * 2 + 1 - zh, ((k // 2) * 4 + x) * 2 + k % 2)
        return 0

    lax.fori_loop(0, NZL * NC, greet_z, 0)

    def greet_xy(k, _):
        greet(lax.rem(y + 1 + k // 4, NY) * 2 + zh, (zl * 4 + k % 4) * 2 + c)
        return 0

    lax.fori_loop(0, (NY - 1) * NX, greet_xy, 0)

    def greet_far(k, _):
        greet(lax.rem(y + k, NY) * 2 + 1 - zh, t)
        return 0

    lax.fori_loop(1, NY, greet_far, 0)

    mine = own[...]
    hot_t = (iota((TENANTS, NT), 0) == mine).astype(F32).astype(BF16)

    def pick(block):
        return lax.dot_general(hot_t, block, (((0,), (0,)), ((), ())), preferred_element_type=F32)

    loads[0].wait()
    loads[1].wait()
    for i in range(8):
        got = pick(fq_v[:, i * 256 : (i + 1) * 256])
        for h in range(2):
            yy, zz = i // 2, i % 2
            gat_q[pl.ds(zz * 8 + yy * 2 + h, NT, stride=32), :] = got[:, h * 128 : (h + 1) * 128]
    got = pick(fv_v[...])
    for h in range(2):
        gat_q[pl.ds(16 + h, NT, stride=32), :] = got[:, h * 128 : (h + 1) * 128]
    for h in range(14):
        gat_q[pl.ds(18 + h, NT, stride=32), :] = jnp.zeros((NT, 128), F32)
    p_qs[...] = gat_q[...].reshape(NT, 32, 128).astype(BF16)
    p_qr[pl.ds(t, 1)] = p_qs[pl.ds(t, 1)]

    own_s[...] = jnp.broadcast_to(jnp.concatenate([mine.astype(F32), jnp.zeros((1, 96), F32)], axis=1), (8, 128))
    own_r[pl.ds(s, 1)] = own_s[...].reshape(1, 8, 128)

    pl.semaphore_wait(bar, (NT - 1) + NZL * NC + (NY - 1) * NX + NY - 1)

    def factor_copy(k, src, dst, send, recv):
        to = lax.rem(t + k, NT)
        return pltpu.make_async_remote_copy(
            src_ref=src.at[to], dst_ref=dst.at[t], send_sem=send.at[k], recv_sem=recv.at[t],
            device_id=(s, to), device_id_type=MESH,
        )

    def factor_arrived(k, dst, send, recv):
        source = lax.rem(t + k, NT)
        pltpu.make_async_remote_copy(
            src_ref=dst.at[source], dst_ref=dst.at[source], send_sem=send.at[k], recv_sem=recv.at[source],
            device_id=(s, source), device_id_type=MESH,
        ).wait_recv()

    def send_q(k, _):
        factor_copy(k, p_qs, p_qr, pq_ss, pq_rs).start()
        return 0

    lax.fori_loop(1, NT, send_q, 0)

    loads[2].wait()
    for i in range(16):
        got = pick(fa_v[:, i * 256 : (i + 1) * 256])
        for h in range(2):
            n = i * 2 + h
            yy, zz, rr = n // 8, (n // 4) % 2, n % 4
            gat_a[pl.ds(zz * 16 + yy * 4 + rr, NT, stride=32), :] = got[:, h * 128 : (h + 1) * 128]
    p_as[...] = gat_a[...].reshape(NT, 32, 128).astype(BF16)
    p_ar[pl.ds(t, 1)] = p_as[pl.ds(t, 1)]

    def send_a(k, _):
        factor_copy(k, p_as, p_ar, pa_ss, pa_rs).start()
        return 0

    lax.fori_loop(1, NT, send_a, 0)

    def own_copy(k):
        to = lax.rem(s + k, NS)
        return pltpu.make_async_remote_copy(
            src_ref=own_s, dst_ref=own_r.at[s], send_sem=own_ss.at[k], recv_sem=own_rs.at[s],
            device_id=(to, t), device_id_type=MESH,
        )

    def send_own(k, _):
        own_copy(k).start()
        return 0

    lax.fori_loop(1, NS, send_own, 0)

    loads[3].wait()

    def turn_q(i, _):
        zl_, c_, xp = i // 4, (i // 2) % 2, i % 2
        base = pl.multiple_of((i % 2) * 512, 512)
        for xi in range(2):
            tt = (zl_ * 4 + xp * 2 + xi) * 2 + c_
            for h in range(2):
                block = gq_v[:, pl.ds(pl.multiple_of(tt * 256 + h * 128, 128), 128)].astype(F32).T
                for yy in range(2):
                    for zz in range(2):
                        tr[pl.ds(base + zz * 256 + xi * 128 + (2 * h + yy) * 32, 32), :] = block[
                            (yy * 2 + zz) * 32 : (yy * 2 + zz + 1) * 32
                        ]
        for zz in range(2):
            row = pl.multiple_of(((zl_ * 2 + zz) * 2 + c_) * 32 + xp * 16, 16)
            for e in range(16):
                b2[pl.ds(row, 16), e * 128 : (e + 1) * 128] = tr[
                    pl.ds(base + zz * 256 + e, 16, stride=16), :
                ].astype(BF16)
        return 0

    lax.fori_loop(0, 16, turn_q, 0, unroll=2)

    loads[4].wait()
    for zl_ in range(4):
        for h in range(2):
            block = gv_v[:, (zl_ * 2 + h) * 128 : (zl_ * 2 + h + 1) * 128].astype(F32).T
            for xx in range(2):
                for c_ in range(2):
                    to = (zl_ * 2 + c_) * 128 + (2 * h + xx) * 32
                    tr[to : to + 32, :] = block[(xx * 2 + c_) * 32 : (xx * 2 + c_ + 1) * 32]
    for g in range(4):
        for e in range(16):
            v2[g * 16 : (g + 1) * 16, e * 128 : (e + 1) * 128] = tr[pl.ds(g * 256 + e, 16, stride=16), :].astype(BF16)

    loads[5].wait()

    def turn_a(i, _):
        base = pl.multiple_of((i % 4) * 256, 256)
        zl_, x_, c_ = i // 8, (i // 2) % 4, i % 2
        for h in range(2):
            block = acts_v[:, pl.ds(pl.multiple_of(i * 256 + h * 128, 128), 128)].astype(F32).T
            for yy in range(2):
                for zz in range(2):
                    tr[pl.ds(base + zz * 128 + (2 * h + yy) * 32, 32), :] = block[
                        (yy * 2 + zz) * 32 : (yy * 2 + zz + 1) * 32
                    ]
        for zz in range(2):
            row = pl.multiple_of((((zl_ * 2 + zz) * 2 + c_) * 4 + x_) * 16, 16)
            for d in range(8):
                a2[pl.ds(row, 16), d * 128 : (d + 1) * 128] = tr[pl.ds(base + zz * 128 + d, 16, stride=8), :].astype(BF16)
        return 0

    lax.fori_loop(0, 32, turn_a, 0, unroll=4)

    def got_q(k, _):
        factor_arrived(k, p_qr, pq_ss, pq_rs)
        return 0

    lax.fori_loop(1, NT, got_q, 0)

    places = [(zl_, zz, c_, x_) for zl_ in range(4) for zz in range(2) for c_ in range(2) for x_ in range(4)]
    backq = jnp.zeros((R, TOK), F32)
    fq_rows = jnp.concatenate(
        [p_qr[(zl_ * 4 + x_) * 2 + c_, 0:16, :].astype(F32)[zz * 8 : (zz + 1) * 8] for zl_, zz, c_, x_ in places], axis=0
    )
    fq_t = fq_rows.T.astype(BF16)
    for n in range(8):
        part = mm(fq_t[n * 16 : (n + 1) * 16], b2[:, n * 256 : (n + 1) * 256])
        backq = backq + part[0:8, 0:128] + part[8:16, 128:256]
    fv_rows = jnp.concatenate(
        [p_qr[(zl_ * 4 + x_) * 2 + c_, 16:32, :].astype(F32)[0:2] for zl_ in range(4) for c_ in range(2) for x_ in range(4)],
        axis=0,
    )
    fv_t = jnp.concatenate([fv_rows, jnp.zeros((64, 128), F32)], axis=0).T.astype(BF16)[:, 0:64]
    backv = jnp.zeros((R, TOK), F32)
    for n in range(8):
        part = mm(fv_t[n * 16 : (n + 1) * 16], v2[:, n * 256 : (n + 1) * 256])
        backv = backv + part[0:8, 0:128] + part[8:16, 128:256]
    back_t = jnp.concatenate([backq, backv], axis=0).astype(BF16).astype(F32)
    back = jnp.concatenate([back_t] * 8, axis=0).T
    lane = iota((TOK, 128), 1)
    diag = jnp.concatenate([jnp.where(lane // 16 == d, back, 0.0).astype(BF16) for d in range(8)], axis=0)

    def z_peer(k):
        q = lax.rem(zdev + k, 16)
        return q, (y * 2 + (q // 2) % 2, ((q // 4) * 4 + x) * 2 + q % 2)

    def z_copy(k, src, dst, send, recv):
        q, device = z_peer(k)
        return pltpu.make_async_remote_copy(
            src_ref=src.at[q], dst_ref=dst.at[zdev], send_sem=send.at[k], recv_sem=recv.at[zdev],
            device_id=device, device_id_type=MESH,
        )

    def z_arrived(k, dst, send, recv):
        q, device = z_peer(k)
        pltpu.make_async_remote_copy(
            src_ref=dst.at[q], dst_ref=dst.at[q], send_sem=send.at[k], recv_sem=recv.at[q],
            device_id=device, device_id_type=MESH,
        ).wait_recv()

    for n in range(4):
        z_as[n * 4 : (n + 1) * 4] = (SCALE * mm(a2[n * 256 : (n + 1) * 256, :], diag)).astype(BF16).reshape(4, 64, 128)

    def send_za(k, _):
        z_copy(k, z_as, z_ar, za_ss, za_rs).start()
        return 0

    lax.fori_loop(1, 16, send_za, 0)
    z_ar[pl.ds(zdev, 1)] = z_as[pl.ds(zdev, 1)]

    def got_a(k, _):
        factor_arrived(k, p_ar, pa_ss, pa_rs)
        return 0

    lax.fori_loop(1, NT, got_a, 0)
    fa_rows = jnp.concatenate([p_ar[(zl_ * 4 + x_) * 2 + c_, zz * 16 : (zz + 1) * 16, :] for zl_, zz, c_, x_ in places], axis=0)
    fa_t = fa_rows.astype(F32).T.astype(BF16)
    down_t = jnp.zeros((2 * R, TOK), F32)
    for n in range(4):
        part = mm(fa_t[n * 32 : (n + 1) * 32], a2[:, n * 256 : (n + 1) * 256])
        down_t = down_t + part[0:16, 0:128] + part[16:32, 128:256]
    down_t = down_t.astype(BF16).astype(F32)
    down_q = jnp.concatenate([down_t[0:8]] * 16, axis=0).T
    down_v = jnp.concatenate([down_t[8:16]] * 16, axis=0).T
    diag_q = jnp.concatenate([jnp.where(lane // 8 == e, down_q, 0.0).astype(BF16) for e in range(16)], axis=0)
    diag_v = jnp.concatenate([jnp.where(lane // 8 == e, down_v, 0.0).astype(BF16) for e in range(16)], axis=0)
    grad_v_rows = SCALE * mm(v2[...], diag_v)
    grad_v_rows = jnp.concatenate(
        [grad_v_rows.reshape(8, 8, 128), jnp.zeros((8, 8, 128), F32)], axis=1
    ).astype(BF16)
    grad_q_rows = (SCALE * mm(b2[...], diag_q)).astype(BF16).reshape(16, 32, 128)
    for q in range(16):
        z_qs[q, 0:32, :] = grad_q_rows[q]
        z_qs[q, 32:48, :] = grad_v_rows[(q // 4) * 2 + q % 2]

    def send_zq(k, _):
        z_copy(k, z_qs, z_qr, zq_ss, zq_rs).start()
        return 0

    lax.fori_loop(1, 16, send_zq, 0)
    z_qr[pl.ds(zdev, 1)] = z_qs[pl.ds(zdev, 1)]

    def got_own(k, _):
        source = lax.rem(s + k, NS)
        pltpu.make_async_remote_copy(
            src_ref=own_s, dst_ref=own_r.at[source], send_sem=own_ss.at[k], recv_sem=own_rs.at[source],
            device_id=(source, t), device_id_type=MESH,
        ).wait_recv()
        return 0

    lax.fori_loop(1, NS, got_own, 0)
    n_seq = NS * NT
    col = iota((1, n_seq), 1)
    col_s = (col // 16 % 4) * 2 + (col // 2) % 2
    col_t = ((col // 4 % 4) * 4 + col // 64) * 2 + col % 2
    owners = jnp.concatenate([own_r[i, 0:1, :] for i in range(NS)], axis=0)
    spread = mm(owners.astype(BF16), (iota((128, n_seq), 0) == col_t).astype(F32).astype(BF16))
    in_section = iota((NS, n_seq), 0) == col_s
    tenant = jnp.sum(jnp.where(in_section, spread, 0.0), axis=0, keepdims=True)
    hot_tenant = (iota((TENANTS, n_seq), 0).astype(F32) == tenant).astype(F32).astype(BF16)
    tasks = jnp.broadcast_to(task_of[...].astype(F32), (8, TENANTS)).astype(BF16)
    task = mm(tasks, hot_tenant)[0:1]
    layers = jnp.broadcast_to(layer_of[...].astype(F32), (NS, NS)).astype(BF16)
    layer = mm(layers, in_section.astype(F32).astype(BF16))[0:1]
    row = iota((TASKS + LAYERS, n_seq), 0).astype(F32)
    hot_head = (row == jnp.where(row < TASKS, task, layer + TASKS)).astype(F32).astype(BF16)
    loads[6].wait()
    loads[7].wait()

    def head_block(i, _):
        at = pl.multiple_of(i * 256, 256)
        v = lax.dot_general(
            emb_v[:, pl.ds(at, 256)], hot_head, (((0,), (0,)), ((), ())), preferred_element_type=F32
        )
        head_v[pl.ds(at, 256), :] = (v / (1.0 + jnp.exp(-v))).astype(BF16)
        return 0

    lax.fori_loop(0, H // 256, head_block, 0)
    share = H // NS
    head_copy = pltpu.make_async_copy(head_v, head_out, out_sem.at[0])
    own_head_copy = pltpu.make_async_copy(
        head_v.at[pl.ds(pl.multiple_of(s * share, share), share)], head_own, out_sem.at[1]
    )
    head_copy.start()
    own_head_copy.start()

    def xy_copy(k, src, dst, send, recv):
        b = lax.rem(xy + k, 16)
        return pltpu.make_async_remote_copy(
            src_ref=src.at[b], dst_ref=dst.at[xy], send_sem=send.at[k], recv_sem=recv.at[xy],
            device_id=((b % 4) * 2 + zh, (zl * 4 + b // 4) * 2 + c), device_id_type=MESH,
        )

    def xy_arrived(k, dst, send, recv):
        b = lax.rem(xy + k, 16)
        pltpu.make_async_remote_copy(
            src_ref=dst.at[b], dst_ref=dst.at[b], send_sem=send.at[k], recv_sem=recv.at[b],
            device_id=((b % 4) * 2 + zh, (zl * 4 + b // 4) * 2 + c), device_id_type=MESH,
        ).wait_recv()

    def got_za(k, _):
        z_arrived(k, z_ar, za_ss, za_rs)
        return 0

    lax.fori_loop(1, 16, got_za, 0)
    big_a[...] = z_ar[...].astype(F32).reshape(1024, 128)
    for b in range(16):
        for i in range(4):
            x_as[b, :, i * 128 : (i + 1) * 128] = big_a[pl.ds(b * 4 + i, 16, stride=64), :].astype(BF16)

    def send_xa(k, _):
        xy_copy(k, x_as, s_a, xa_ss, xa_rs).start()
        return 0

    lax.fori_loop(1, 16, send_xa, 0)
    s_a[pl.ds(xy, 1)] = x_as[pl.ds(xy, 1)]

    def got_zq(k, _):
        z_arrived(k, z_qr, zq_ss, zq_rs)
        return 0

    lax.fori_loop(1, 16, got_zq, 0)
    big_q[...] = z_qr[...].astype(F32).reshape(768, 128)
    for b in range(16):
        for i in range(2):
            x_qs[b, :, i * 128 : (i + 1) * 128] = big_q[pl.ds(b * 2 + i, 16, stride=48), :].astype(BF16)
            x_qs[b, :, 256 + i * 128 : 256 + (i + 1) * 128] = big_q[
                pl.ds(32 + (b // 4) * 2 + i, 16, stride=48), :
            ].astype(BF16)

    def send_xq(k, _):
        xy_copy(k, x_qs, s_q, xq_ss, xq_rs).start()
        return 0

    lax.fori_loop(1, 16, send_xq, 0)
    s_q[pl.ds(xy, 1)] = x_qs[pl.ds(xy, 1)]

    def sent_factors(k, _):
        factor_copy(k, p_qs, p_qr, pq_ss, pq_rs).wait_send()
        factor_copy(k, p_as, p_ar, pa_ss, pa_rs).wait_send()
        return 0

    lax.fori_loop(1, NT, sent_factors, 0)

    def sent_own(k, _):
        own_copy(k).wait_send()
        return 0

    lax.fori_loop(1, NS, sent_own, 0)

    def sent_z(k, _):
        z_copy(k, z_as, z_ar, za_ss, za_rs).wait_send()
        z_copy(k, z_qs, z_qr, zq_ss, zq_rs).wait_send()
        return 0

    lax.fori_loop(1, 16, sent_z, 0)
    head_copy.wait()
    own_head_copy.wait()

    def done_xy(k, _):
        xy_arrived(k, s_a, xa_ss, xa_rs)
        xy_arrived(k, s_q, xq_ss, xq_rs)
        xy_copy(k, x_as, s_a, xa_ss, xa_rs).wait_send()
        xy_copy(k, x_qs, s_q, xq_ss, xq_rs).wait_send()
        return 0

    lax.fori_loop(1, 16, done_xy, 0)


def head_product(head, s_a, s_q, head_own, grad_a, grad_bq, grad_bv):
    rows = head[...]
    grad_a[...] = mm(rows, s_a[...]).astype(BF16)
    grad_bq[...] = mm(rows, s_q[:, 0:256]).astype(BF16)

    @pl.when(pl.program_id(0) == 0)
    def _():
        grad_bv[...] = mm(head_own[...], s_q[:, 256:512]).astype(BF16)


def shards(acts, grad_q, grad_v, fac_a, fac_bq, fac_bv, seq_tenant, tenant_task, section_layer, task_emb, layer_emb):
    vmem = pl.BlockSpec(memory_space=pltpu.VMEM)
    anywhere = pl.BlockSpec(memory_space=pl.ANY)
    dma = pltpu.SemaphoreType.DMA
    s_a, s_q, head, head_own = pl.pallas_call(
        exchange,
        out_shape=(
            jax.ShapeDtypeStruct((16, 16, 512), BF16),
            jax.ShapeDtypeStruct((16, 16, 512), BF16),
            jax.ShapeDtypeStruct((H, NS * NT), BF16),
            jax.ShapeDtypeStruct((H // NS, NS * NT), BF16),
        ),
        in_specs=[anywhere] * 6 + [vmem] * 3 + [anywhere] * 2,
        out_specs=(vmem, vmem, anywhere, anywhere),
        scratch_shapes=[
            pltpu.VMEM((TOK, 8192), BF16),
            pltpu.VMEM((TOK, 8192), BF16),
            pltpu.VMEM((TOK, 1024), BF16),
            pltpu.VMEM((TENANTS, 4096), BF16),
            pltpu.VMEM((TENANTS, 2048), BF16),
            pltpu.VMEM((TENANTS, 256), BF16),
            pltpu.VMEM((TASKS + LAYERS, H), BF16),
            pltpu.VMEM((H, NS * NT), BF16),
            pltpu.VMEM((8, 128), F32),
            pltpu.VMEM((NS, 8, 128), F32),
            pltpu.VMEM((NT * 32, 128), F32),
            pltpu.VMEM((NT * 32, 128), F32),
            pltpu.VMEM((1024, 128), F32),
            pltpu.VMEM((1024, 1024), BF16),
            pltpu.VMEM((512, 2048), BF16),
            pltpu.VMEM((64, 2048), BF16),
            pltpu.VMEM((NT, 32, 128), BF16),
            pltpu.VMEM((NT, 32, 128), BF16),
            pltpu.VMEM((NT, 32, 128), BF16),
            pltpu.VMEM((NT, 32, 128), BF16),
            pltpu.VMEM((16, 64, 128), BF16),
            pltpu.VMEM((16, 64, 128), BF16),
            pltpu.VMEM((16, 48, 128), BF16),
            pltpu.VMEM((16, 48, 128), BF16),
            pltpu.VMEM((16, 16, 512), BF16),
            pltpu.VMEM((16, 16, 512), BF16),
            pltpu.VMEM((1024, 128), F32),
            pltpu.VMEM((768, 128), F32),
            dma((8,)), dma((2,)),
            dma((NS,)), dma((NS,)),
            dma((NT,)), dma((NT,)), dma((NT,)), dma((NT,)),
            dma((16,)), dma((16,)), dma((16,)), dma((16,)),
            dma((16,)), dma((16,)), dma((16,)), dma((16,)),
        ],
        compiler_params=pltpu.CompilerParams(
            collective_id=0, has_side_effects=True, vmem_limit_bytes=56 * 1024 * 1024
        ),
        name="exchange",
    )(
        acts[0], grad_q[0], grad_v[0], fac_a[0], fac_bq[0], fac_bv[0], seq_tenant,
        tenant_task.reshape(1, TENANTS), section_layer.reshape(1, NS), task_emb, layer_emb,
    )
    tile = 512
    return pl.pallas_call(
        head_product,
        grid=(H // tile,),
        out_shape=(
            jax.ShapeDtypeStruct((H, 512), BF16),
            jax.ShapeDtypeStruct((H, 256), BF16),
            jax.ShapeDtypeStruct((H // NS, 256), BF16),
        ),
        in_specs=[
            pl.BlockSpec((tile, 256), lambda i: (i, 0)),
            pl.BlockSpec((256, 512), lambda i: (0, 0)),
            pl.BlockSpec((256, 512), lambda i: (0, 0)),
            pl.BlockSpec((512, 256), lambda i: (0, 0)),
        ],
        out_specs=(
            pl.BlockSpec((tile, 512), lambda i: (i, 0)),
            pl.BlockSpec((tile, 256), lambda i: (i, 0)),
            pl.BlockSpec((512, 256), lambda i: (0, 0)),
        ),
        compiler_params=pltpu.CompilerParams(vmem_limit_bytes=60 * 1024 * 1024),
        name="head_product",
    )(head, s_a.reshape(256, 512), s_q.reshape(256, 512), head_own)


def solution(mesh):
    placed = (
        P("section", "tensor", None),
        P("section", "tensor", None),
        P("section", "tensor", None),
        P("section", None, "tensor"),
        P("section", None, "tensor"),
        P("section", None, "tensor"),
        P("section", None),
        P(),
        P(),
        P(),
        P(),
    )
    return jax.shard_map(
        shards,
        mesh=mesh,
        in_specs=placed,
        out_specs=(
            P(None, ("tensor", "section")),
            P(None, ("tensor", "section")),
            P("section", "tensor"),
        ),
        check_vma=False,
    )
```

time: 290 us -> 57.2 us (0.20)
  the two profiles are of different devices: /device:TPU:66 before, /device:TPU:1 now
where the time goes in v1:
time: 57.2 us; the launch traced here: 56.9 us
  Pallas kernels  56.3 us (98%)
  between operations  0.64 us (1%)
    pallas_call x1, Pallas kernels, shards(): pl.pallas_call(exchange, out_shape=(jax.ShapeDtypeStruct((16, 16, 512), B...  48.1 us
    pallas_call x1, Pallas kernels, shards(): pl.pallas_call(head_product, grid=(H // tile,), out_shape=(jax.ShapeDtype...  8.22 us

profile of v1, /device:TPU:1, one launch (start us, length us, event | category | flops | bytes accessed | tf_op | source)
XLA Modules:
  0.0 56.9 jit_solution(18255246127817045557)
XLA Ops:
  0.6 48.1 %exchange.1 = (bf16[16,16,512]{2,1,0:T(8,128)(2,1)}, bf16[16,16,512]{2,1,0:T(8,128)(2,1)}, bf16[4096,256]{1,0:T(8,128)(2,1)}, bf16[512,256]{1,0:T(8,128)(2,1)}) custom-call(bf16[128,8192]{1,0:T(8,128)(2,1)} %bitcast.10, bf16[128,8192]{1,0:T(8,128)(2,1)} %bitcast.11, bf16[128,1024]{1,0:T(8,128)(2,1)} %bitcast.14, bf16[128,4096]{1,0:T(8,128)(2,1)} %bitcast.12, ...), custom_call_target="tpu_custom_call" | custom-call | tf_op jit(solution)/shard_map/exchange/pallas_call | solution.py:450
  48.7 8.2 %head_product.1 = (bf16[4096,512]{1,0:T(8,128)(2,1)}, bf16[4096,256]{1,0:T(8,128)(2,1)}, bf16[512,256]{1,0:T(8,128)(2,1)}) custom-call(bf16[4096,256]{1,0:T(8,128)(2,1)} %get-tuple-element.7.head, bf16[256,512]{1,0:T(8,128)(2,1)} %bitcast.15, bf16[256,512]{1,0:T(8,128)(2,1)} %bitcast.16, bf16[512,256]{1,0:T(8,128)(2,1)} %get-tuple-element.10.head_own), custom_call_target="tpu_custom_call" | custom-call | tf_op jit(solution)/shard_map/head_product/pallas_call | solution.py:504

commit v2 on v1

--- a/solution.py
+++ b/solution.py
@@ -19,6 +19,8 @@
 TOK = 128
 NS, NT = 8, 32
 NX, NY, NZL, NZH, NC = 4, 4, 4, 2, 2
+HEAD_FIRST = 8
+PIECES = 4
 SCALE = 2.0 / math.sqrt(TOK * NT * NS)
 
 
@@ -32,11 +34,11 @@
 
 def exchange(
     acts, gq, gv, fa, fq, fv, own, task_of, layer_of, task_emb, layer_emb,
-    s_a, s_q, head_out, head_own,
-    acts_v, gq_v, gv_v, fa_v, fq_v, fv_v, emb_v, head_v,
+    s_a, s_q, head, head_own,
+    acts_v, gq_v, gv_v, fa_v, fq_v, fv_v, emb_v, own_v, task_v, layer_v,
     own_s, own_r, gat_a, gat_q, tr, a2, b2, v2,
     p_as, p_ar, p_qs, p_qr, z_as, z_ar, z_qs, z_qr, x_as, x_qs, big_a, big_q,
-    load_sem, out_sem, own_ss, own_rs, pa_ss, pa_rs, pq_ss, pq_rs, za_ss, za_rs, zq_ss, zq_rs, xa_ss, xa_rs, xq_ss, xq_rs,
+    load_sem, own_ss, own_rs, pa_ss, pa_rs, pq_ss, pq_rs, za_ss, za_rs, zq_ss, zq_rs, xa_ss, xa_rs, xq_ss, xq_rs,
 ):
     s, t = lax.axis_index("section"), lax.axis_index("tensor")
     y, zh = s // 2, s % 2
@@ -44,67 +46,69 @@
     zdev = (zl * 2 + zh) * 2 + c
     xy = x * 4 + y
 
+    bar = pltpu.get_barrier_semaphore()
+
+    def greet(section, tensor):
+        pl.semaphore_signal(bar, inc=1, device_id=(section, tensor), device_id_type=MESH)
+
+    def greet_tensor(k, _):
+        greet(s, lax.rem(t + k, NT))
+        return 0
+
+    lax.fori_loop(1, NT, greet_tensor, 0)
+
+    def greet_z(k, _):
+        greet(y * 2 + 1 - zh, ((k // 2) * 4 + x) * 2 + k % 2)
+        return 0
+
+    lax.fori_loop(0, NZL * NC, greet_z, 0)
+
+    def greet_xy(k, _):
+        greet(lax.rem(y + 1 + k // 4, NY) * 2 + zh, (zl * 4 + k % 4) * 2 + c)
+        return 0
+
+    lax.fori_loop(0, (NY - 1) * NX, greet_xy, 0)
+
+    def greet_far(k, _):
+        greet(lax.rem(y + k, NY) * 2 + 1 - zh, t)
+        return 0
+
+    lax.fori_loop(1, NY, greet_far, 0)
+
     loads = [
         pltpu.make_async_copy(src, dst, load_sem.at[i])
         for i, (src, dst) in enumerate(
             (
-                (fq, fq_v), (fv, fv_v), (fa, fa_v), (gq, gq_v), (gv, gv_v), (acts, acts_v),
+                (own, own_v), (fq, fq_v), (fv, fv_v), (fa, fa_v), (gq, gq_v), (gv, gv_v), (acts, acts_v),
                 (task_emb, emb_v.at[pl.ds(0, TASKS)]),
                 (layer_emb, emb_v.at[pl.ds(TASKS, LAYERS)]),
+                (task_of, task_v), (layer_of, layer_v),
             )
         )
     ]
     for load in loads:
         load.start()
 
-    bar = pltpu.get_barrier_semaphore()
-
-    def greet(section, tensor):
-        pl.semaphore_signal(bar, inc=1, device_id=(section, tensor), device_id_type=MESH)
-
-    def greet_tensor(k, _):
-        greet(s, lax.rem(t + k, NT))
-        return 0
-
-    lax.fori_loop(1, NT, greet_tensor, 0)
-
-    def greet_z(k, _):
-        greet(y * 2 + 1 - zh, ((k // 2) * 4 + x) * 2 + k % 2)
-        return 0
-
-    lax.fori_loop(0, NZL * NC, greet_z, 0)
-
-    def greet_xy(k, _):
-        greet(lax.rem(y + 1 + k // 4, NY) * 2 + zh, (zl * 4 + k % 4) * 2 + c)
-        return 0
-
-    lax.fori_loop(0, (NY - 1) * NX, greet_xy, 0)
-
-    def greet_far(k, _):
-        greet(lax.rem(y + k, NY) * 2 + 1 - zh, t)
-        return 0
-
-    lax.fori_loop(1, NY, greet_far, 0)
-
-    mine = own[...]
+    loads[0].wait()
+    mine = own_v[...]
     hot_t = (iota((TENANTS, NT), 0) == mine).astype(F32).astype(BF16)
 
     def pick(block):
         return lax.dot_general(hot_t, block, (((0,), (0,)), ((), ())), preferred_element_type=F32)
 
-    loads[0].wait()
     loads[1].wait()
+    loads[2].wait()
     for i in range(8):
         got = pick(fq_v[:, i * 256 : (i + 1) * 256])
         for h in range(2):
             yy, zz = i // 2, i % 2
-            gat_q[pl.ds(zz * 8 + yy * 2 + h, NT, stride=32), :] = got[:, h * 128 : (h + 1) * 128]
+            gat_q[pl.ds(zz * 8 + yy * 2 + h, NT, stride=24), :] = got[:, h * 128 : (h + 1) * 128]
     got = pick(fv_v[...])
     for h in range(2):
-        gat_q[pl.ds(16 + h, NT, stride=32), :] = got[:, h * 128 : (h + 1) * 128]
-    for h in range(14):
-        gat_q[pl.ds(18 + h, NT, stride=32), :] = jnp.zeros((NT, 128), F32)
-    p_qs[...] = gat_q[...].reshape(NT, 32, 128).astype(BF16)
+        gat_q[pl.ds(16 + h, NT, stride=24), :] = got[:, h * 128 : (h + 1) * 128]
+    for h in range(6):
+        gat_q[pl.ds(18 + h, NT, stride=24), :] = jnp.zeros((NT, 128), F32)
+    p_qs[...] = gat_q[...].reshape(NT, 24, 128).astype(BF16)
     p_qr[pl.ds(t, 1)] = p_qs[pl.ds(t, 1)]
 
     own_s[...] = jnp.broadcast_to(jnp.concatenate([mine.astype(F32), jnp.zeros((1, 96), F32)], axis=1), (8, 128))
@@ -126,13 +130,26 @@
             device_id=(s, source), device_id_type=MESH,
         ).wait_recv()
 
+    def own_copy(k):
+        to = lax.rem(s + k, NS)
+        return pltpu.make_async_remote_copy(
+            src_ref=own_s, dst_ref=own_r.at[s], send_sem=own_ss.at[k], recv_sem=own_rs.at[s],
+            device_id=(to, t), device_id_type=MESH,
+        )
+
+    def send_own(k, _):
+        own_copy(k).start()
+        return 0
+
+    lax.fori_loop(1, NS, send_own, 0)
+
     def send_q(k, _):
         factor_copy(k, p_qs, p_qr, pq_ss, pq_rs).start()
         return 0
 
     lax.fori_loop(1, NT, send_q, 0)
 
-    loads[2].wait()
+    loads[3].wait()
     for i in range(16):
         got = pick(fa_v[:, i * 256 : (i + 1) * 256])
         for h in range(2):
@@ -148,20 +165,7 @@
 
     lax.fori_loop(1, NT, send_a, 0)
 
-    def own_copy(k):
-        to = lax.rem(s + k, NS)
-        return pltpu.make_async_remote_copy(
-            src_ref=own_s, dst_ref=own_r.at[s], send_sem=own_ss.at[k], recv_sem=own_rs.at[s],
-            device_id=(to, t), device_id_type=MESH,
-        )
-
-    def send_own(k, _):
-        own_copy(k).start()
-        return 0
-
-    lax.fori_loop(1, NS, send_own, 0)
-
-    loads[3].wait()
+    loads[4].wait()
 
     def turn_q(i, _):
         zl_, c_, xp = i // 4, (i // 2) % 2, i % 2
@@ -185,7 +189,7 @@
 
     lax.fori_loop(0, 16, turn_q, 0, unroll=2)
 
-    loads[4].wait()
+    loads[5].wait()
     for zl_ in range(4):
         for h in range(2):
             block = gv_v[:, (zl_ * 2 + h) * 128 : (zl_ * 2 + h + 1) * 128].astype(F32).T
@@ -197,7 +201,7 @@
         for e in range(16):
             v2[g * 16 : (g + 1) * 16, e * 128 : (e + 1) * 128] = tr[pl.ds(g * 256 + e, 16, stride=16), :].astype(BF16)
 
-    loads[5].wait()
+    loads[6].wait()
 
     def turn_a(i, _):
         base = pl.multiple_of((i % 4) * 256, 256)
@@ -233,7 +237,7 @@
         part = mm(fq_t[n * 16 : (n + 1) * 16], b2[:, n * 256 : (n + 1) * 256])
         backq = backq + part[0:8, 0:128] + part[8:16, 128:256]
     fv_rows = jnp.concatenate(
-        [p_qr[(zl_ * 4 + x_) * 2 + c_, 16:32, :].astype(F32)[0:2] for zl_ in range(4) for c_ in range(2) for x_ in range(4)],
+        [p_qr[(zl_ * 4 + x_) * 2 + c_, 16:24, :].astype(F32)[0:2] for zl_ in range(4) for c_ in range(2) for x_ in range(4)],
         axis=0,
     )
     fv_t = jnp.concatenate([fv_rows, jnp.zeros((64, 128), F32)], axis=0).T.astype(BF16)[:, 0:64]
@@ -273,6 +277,43 @@
 
     lax.fori_loop(1, 16, send_za, 0)
     z_ar[pl.ds(zdev, 1)] = z_as[pl.ds(zdev, 1)]
+
+    def got_own(k, _):
+        source = lax.rem(s + k, NS)
+        pltpu.make_async_remote_copy(
+            src_ref=own_s, dst_ref=own_r.at[source], send_sem=own_ss.at[k], recv_sem=own_rs.at[source],
+            device_id=(source, t), device_id_type=MESH,
+        ).wait_recv()
+        return 0
+
+    lax.fori_loop(1, NS, got_own, 0)
+    for i in (7, 8, 9, 10):
+        loads[i].wait()
+    n_seq = NS * NT
+    col = iota((1, n_seq), 1)
+    col_s = (col // 16 % 4) * 2 + (col // 2) % 2
+    col_t = ((col // 4 % 4) * 4 + col // 64) * 2 + col % 2
+    owners = jnp.concatenate([own_r[i, 0:1, :] for i in range(NS)], axis=0)
+    spread = mm(owners.astype(BF16), (iota((128, n_seq), 0) == col_t).astype(F32).astype(BF16))
+    in_section = iota((NS, n_seq), 0) == col_s
+    tenant = jnp.sum(jnp.where(in_section, spread, 0.0), axis=0, keepdims=True)
+    hot_tenant = (iota((TENANTS, n_seq), 0).astype(F32) == tenant).astype(F32).astype(BF16)
+    tasks = jnp.broadcast_to(task_v[...].astype(F32), (8, TENANTS)).astype(BF16)
+    task = mm(tasks, hot_tenant)[0:1]
+    layers = jnp.broadcast_to(layer_v[...].astype(F32), (NS, NS)).astype(BF16)
+    layer = mm(layers, in_section.astype(F32).astype(BF16))[0:1]
+    row = iota((TASKS + LAYERS, n_seq), 0).astype(F32)
+    hot_head = (row == jnp.where(row < TASKS, task, layer + TASKS)).astype(F32).astype(BF16)
+
+    def head_block(i, _):
+        at = pl.multiple_of(i * 256, 256)
+        v = lax.dot_general(
+            emb_v[:, pl.ds(at, 256)], hot_head, (((0,), (0,)), ((), ())), preferred_element_type=F32
+        )
+        head[pl.ds(at, 256), :] = (v / (1.0 + jnp.exp(-v))).astype(BF16)
+        return 0
+
+    lax.fori_loop(0, HEAD_FIRST, head_block, 0)
 
     def got_a(k, _):
         factor_arrived(k, p_ar, pa_ss, pa_rs)
@@ -291,13 +332,11 @@
     diag_q = jnp.concatenate([jnp.where(lane // 8 == e, down_q, 0.0).astype(BF16) for e in range(16)], axis=0)
     diag_v = jnp.concatenate([jnp.where(lane // 8 == e, down_v, 0.0).astype(BF16) for e in range(16)], axis=0)
     grad_v_rows = SCALE * mm(v2[...], diag_v)
-    grad_v_rows = jnp.concatenate(
-        [grad_v_rows.reshape(8, 8, 128), jnp.zeros((8, 8, 128), F32)], axis=1
-    ).astype(BF16)
+    grad_v_rows = grad_v_rows.reshape(8, 8, 128).astype(BF16)
     grad_q_rows = (SCALE * mm(b2[...], diag_q)).astype(BF16).reshape(16, 32, 128)
     for q in range(16):
         z_qs[q, 0:32, :] = grad_q_rows[q]
-        z_qs[q, 32:48, :] = grad_v_rows[(q // 4) * 2 + q % 2]
+        z_qs[q, 32:40, :] = grad_v_rows[(q // 4) * 2 + q % 2]
 
     def send_zq(k, _):
         z_copy(k, z_qs, z_qr, zq_ss, zq_rs).start()
@@ -306,49 +345,9 @@
     lax.fori_loop(1, 16, send_zq, 0)
     z_qr[pl.ds(zdev, 1)] = z_qs[pl.ds(zdev, 1)]
 
-    def got_own(k, _):
-        source = lax.rem(s + k, NS)
-        pltpu.make_async_remote_copy(
-            src_ref=own_s, dst_ref=own_r.at[source], send_sem=own_ss.at[k], recv_sem=own_rs.at[source],
-            device_id=(source, t), device_id_type=MESH,
-        ).wait_recv()
-        return 0
-
-    lax.fori_loop(1, NS, got_own, 0)
-    n_seq = NS * NT
-    col = iota((1, n_seq), 1)
-    col_s = (col // 16 % 4) * 2 + (col // 2) % 2
-    col_t = ((col // 4 % 4) * 4 + col // 64) * 2 + col % 2
-    owners = jnp.concatenate([own_r[i, 0:1, :] for i in range(NS)], axis=0)
-    spread = mm(owners.astype(BF16), (iota((128, n_seq), 0) == col_t).astype(F32).astype(BF16))
-    in_section = iota((NS, n_seq), 0) == col_s
-    tenant = jnp.sum(jnp.where(in_section, spread, 0.0), axis=0, keepdims=True)
-    hot_tenant = (iota((TENANTS, n_seq), 0).astype(F32) == tenant).astype(F32).astype(BF16)
-    tasks = jnp.broadcast_to(task_of[...].astype(F32), (8, TENANTS)).astype(BF16)
-    task = mm(tasks, hot_tenant)[0:1]
-    layers = jnp.broadcast_to(layer_of[...].astype(F32), (NS, NS)).astype(BF16)
-    layer = mm(layers, in_section.astype(F32).astype(BF16))[0:1]
-    row = iota((TASKS + LAYERS, n_seq), 0).astype(F32)
-    hot_head = (row == jnp.where(row < TASKS, task, layer + TASKS)).astype(F32).astype(BF16)
-    loads[6].wait()
-    loads[7].wait()
-
-    def head_block(i, _):
-        at = pl.multiple_of(i * 256, 256)
-        v = lax.dot_general(
-            emb_v[:, pl.ds(at, 256)], hot_head, (((0,), (0,)), ((), ())), preferred_element_type=F32
-        )
-        head_v[pl.ds(at, 256), :] = (v / (1.0 + jnp.exp(-v))).astype(BF16)
-        return 0
-
-    lax.fori_loop(0, H // 256, head_block, 0)
+    lax.fori_loop(HEAD_FIRST, H // 256, head_block, 0)
     share = H // NS
-    head_copy = pltpu.make_async_copy(head_v, head_out, out_sem.at[0])
-    own_head_copy = pltpu.make_async_copy(
-        head_v.at[pl.ds(pl.multiple_of(s * share, share), share)], head_own, out_sem.at[1]
-    )
-    head_copy.start()
-    own_head_copy.start()
+    head_own[...] = head[pl.ds(pl.multiple_of(s * share, share), share), :]
 
     def xy_copy(k, src, dst, send, recv):
         b = lax.rem(xy + k, 16)
@@ -386,12 +385,12 @@
         return 0
 
     lax.fori_loop(1, 16, got_zq, 0)
-    big_q[...] = z_qr[...].astype(F32).reshape(768, 128)
+    big_q[...] = z_qr[...].astype(F32).reshape(640, 128)
     for b in range(16):
         for i in range(2):
-            x_qs[b, :, i * 128 : (i + 1) * 128] = big_q[pl.ds(b * 2 + i, 16, stride=48), :].astype(BF16)
+            x_qs[b, :, i * 128 : (i + 1) * 128] = big_q[pl.ds(b * 2 + i, 16, stride=40), :].astype(BF16)
             x_qs[b, :, 256 + i * 128 : 256 + (i + 1) * 128] = big_q[
-                pl.ds(32 + (b // 4) * 2 + i, 16, stride=48), :
+                pl.ds(32 + (b // 4) * 2 + i, 16, stride=40), :
             ].astype(BF16)
 
     def send_xq(k, _):
@@ -420,8 +419,6 @@
         return 0
 
     lax.fori_loop(1, 16, sent_z, 0)
-    head_copy.wait()
-    own_head_copy.wait()
 
     def done_xy(k, _):
         xy_arrived(k, s_a, xa_ss, xa_rs)
@@ -433,30 +430,46 @@
     lax.fori_loop(1, 16, done_xy, 0)
 
 
-def head_product(head, s_a, s_q, head_own, grad_a, grad_bq, grad_bv):
-    rows = head[...]
-    grad_a[...] = mm(rows, s_a[...]).astype(BF16)
-    grad_bq[...] = mm(rows, s_q[:, 0:256]).astype(BF16)
-
-    @pl.when(pl.program_id(0) == 0)
-    def _():
-        grad_bv[...] = mm(head_own[...], s_q[:, 256:512]).astype(BF16)
+def head_product(head, s_a, s_q, head_own, grad_a, grad_bq, grad_bv, a_v, q_v, v_v, sem):
+    copies = []
+
+    def write(src, dst, rows):
+        copy = pltpu.make_async_copy(src.at[rows], dst.at[rows], sem.at[len(copies)])
+        copy.start()
+        copies.append(copy)
+
+    step = H // PIECES
+    for p in range(PIECES):
+        for r in range(p * step, (p + 1) * step, 256):
+            a_v[r : r + 256, :] = mm(head[r : r + 256, :], s_a[...]).astype(BF16)
+        write(a_v, grad_a, pl.ds(p * step, step))
+        for r in range(p * step, (p + 1) * step, 256):
+            q_v[r : r + 256, :] = mm(head[r : r + 256, :], s_q[:, 0:256]).astype(BF16)
+        write(q_v, grad_bq, pl.ds(p * step, step))
+    v_v[...] = mm(head_own[...], s_q[:, 256:512]).astype(BF16)
+    write(v_v, grad_bv, pl.ds(0, H // NS))
+    for copy in copies:
+        copy.wait()
 
 
 def shards(acts, grad_q, grad_v, fac_a, fac_bq, fac_bv, seq_tenant, tenant_task, section_layer, task_emb, layer_emb):
     vmem = pl.BlockSpec(memory_space=pltpu.VMEM)
-    anywhere = pl.BlockSpec(memory_space=pl.ANY)
+    hbm = pl.BlockSpec(memory_space=pltpu.HBM)
     dma = pltpu.SemaphoreType.DMA
+    inputs = (
+        acts[0], grad_q[0], grad_v[0], fac_a[0], fac_bq[0], fac_bv[0], seq_tenant,
+        tenant_task.reshape(1, TENANTS), section_layer.reshape(1, NS), task_emb, layer_emb,
+    )
     s_a, s_q, head, head_own = pl.pallas_call(
         exchange,
         out_shape=(
-            jax.ShapeDtypeStruct((16, 16, 512), BF16),
-            jax.ShapeDtypeStruct((16, 16, 512), BF16),
-            jax.ShapeDtypeStruct((H, NS * NT), BF16),
-            jax.ShapeDtypeStruct((H // NS, NS * NT), BF16),
+            pltpu.VMEM((16, 16, 512), BF16),
+            pltpu.VMEM((16, 16, 512), BF16),
+            pltpu.VMEM((H, NS * NT), BF16),
+            pltpu.VMEM((H // NS, NS * NT), BF16),
         ),
-        in_specs=[anywhere] * 6 + [vmem] * 3 + [anywhere] * 2,
-        out_specs=(vmem, vmem, anywhere, anywhere),
+        in_specs=[hbm] * len(inputs),
+        out_specs=(vmem,) * 4,
         scratch_shapes=[
             pltpu.VMEM((TOK, 8192), BF16),
             pltpu.VMEM((TOK, 8192), BF16),
@@ -465,62 +478,56 @@
             pltpu.VMEM((TENANTS, 2048), BF16),
             pltpu.VMEM((TENANTS, 256), BF16),
             pltpu.VMEM((TASKS + LAYERS, H), BF16),
-            pltpu.VMEM((H, NS * NT), BF16),
+            pltpu.VMEM((1, NT), jnp.int32),
+            pltpu.VMEM((1, TENANTS), jnp.int32),
+            pltpu.VMEM((1, NS), jnp.int32),
             pltpu.VMEM((8, 128), F32),
             pltpu.VMEM((NS, 8, 128), F32),
             pltpu.VMEM((NT * 32, 128), F32),
-            pltpu.VMEM((NT * 32, 128), F32),
+            pltpu.VMEM((NT * 24, 128), F32),
             pltpu.VMEM((1024, 128), F32),
             pltpu.VMEM((1024, 1024), BF16),
             pltpu.VMEM((512, 2048), BF16),
             pltpu.VMEM((64, 2048), BF16),
             pltpu.VMEM((NT, 32, 128), BF16),
             pltpu.VMEM((NT, 32, 128), BF16),
-            pltpu.VMEM((NT, 32, 128), BF16),
-            pltpu.VMEM((NT, 32, 128), BF16),
+            pltpu.VMEM((NT, 24, 128), BF16),
+            pltpu.VMEM((NT, 24, 128), BF16),
             pltpu.VMEM((16, 64, 128), BF16),
             pltpu.VMEM((16, 64, 128), BF16),
-            pltpu.VMEM((16, 48, 128), BF16),
-            pltpu.VMEM((16, 48, 128), BF16),
+            pltpu.VMEM((16, 40, 128), BF16),
+            pltpu.VMEM((16, 40, 128), BF16),
             pltpu.VMEM((16, 16, 512), BF16),
             pltpu.VMEM((16, 16, 512), BF16),
             pltpu.VMEM((1024, 128), F32),
-            pltpu.VMEM((768, 128), F32),
-            dma((8,)), dma((2,)),
+            pltpu.VMEM((640, 128), F32),
+            dma((len(inputs),)),
             dma((NS,)), dma((NS,)),
             dma((NT,)), dma((NT,)), dma((NT,)), dma((NT,)),
             dma((16,)), dma((16,)), dma((16,)), dma((16,)),
             dma((16,)), dma((16,)), dma((16,)), dma((16,)),
         ],
         compiler_params=pltpu.CompilerParams(
-            collective_id=0, has_side_effects=True, vmem_limit_bytes=56 * 1024 * 1024
+            collective_id=0, has_side_effects=True, vmem_limit_bytes=36 * 1024 * 1024
         ),
         name="exchange",
-    )(
-        acts[0], grad_q[0], grad_v[0], fac_a[0], fac_bq[0], fac_bv[0], seq_tenant,
-        tenant_task.reshape(1, TENANTS), section_layer.reshape(1, NS), task_emb, layer_emb,
-    )
-    tile = 512
+    )(*(pltpu.with_memory_space_constraint(a, pltpu.HBM) for a in inputs))
     return pl.pallas_call(
         head_product,
-        grid=(H // tile,),
         out_shape=(
             jax.ShapeDtypeStruct((H, 512), BF16),
             jax.ShapeDtypeStruct((H, 256), BF16),
             jax.ShapeDtypeStruct((H // NS, 256), BF16),
         ),
-        in_specs=[
-            pl.BlockSpec((tile, 256), lambda i: (i, 0)),
-            pl.BlockSpec((256, 512), lambda i: (0, 0)),
-            pl.BlockSpec((256, 512), lambda i: (0, 0)),
-            pl.BlockSpec((512, 256), lambda i: (0, 0)),
+        in_specs=[vmem] * 4,
+        out_specs=(hbm,) * 3,
+        scratch_shapes=[
+            pltpu.VMEM((H, 512), BF16),
+            pltpu.VMEM((H, 256), BF16),
+            pltpu.VMEM((H // NS, 256), BF16),
+            dma((2 * PIECES + 1,)),
         ],
-        out_specs=(
-            pl.BlockSpec((tile, 512), lambda i: (i, 0)),
-            pl.BlockSpec((tile, 256), lambda i: (i, 0)),
-            pl.BlockSpec((512, 256), lambda i: (0, 0)),
-        ),
-        compiler_params=pltpu.CompilerParams(vmem_limit_bytes=60 * 1024 * 1024),
+        compiler_params=pltpu.CompilerParams(vmem_limit_bytes=20 * 1024 * 1024),
         name="head_product",
     )(head, s_a.reshape(256, 512), s_q.reshape(256, 512), head_own)
 

time: 57.2 us -> 48.1 us (0.84)
  Pallas kernels: 56.3 us -> 47.4 us
    pallas_call x2, Pallas kernels: 56.3 us -> 47.4 us  [the longest x1 44.1 us: shards(): pl.pallas_call(exchange, out_shape=(pltpu.VMEM((16, 16, 512), BF16), pltp...]
where the time goes in v2:
time: 48.1 us; the launch traced here: 48 us
  Pallas kernels  47.4 us (99%)
  between operations  0.64 us (1%)
    pallas_call x1, Pallas kernels, shards(): pl.pallas_call(exchange, out_shape=(pltpu.VMEM((16, 16, 512), BF16), pltp...  44.1 us
    pallas_call x1, Pallas kernels, shards(): pl.pallas_call(head_product, out_shape=(jax.ShapeDtypeStruct((H, 512), BF...  3.3 us

profile of v2, /device:TPU:1, one launch (start us, length us, event | category | flops | bytes accessed | tf_op | source)
XLA Modules:
  0.0 48.0 jit_solution(493120759071330380)
XLA Ops:
  0.6 44.1 %exchange.1 = (bf16[16,16,512]{2,1,0:T(8,128)(2,1)S(1)}, bf16[16,16,512]{2,1,0:T(8,128)(2,1)S(1)}, bf16[4096,256]{1,0:T(8,128)(2,1)S(1)}, bf16[512,256]{1,0:T(8,128)(2,1)S(1)}) custom-call(bf16[128,8192]{1,0:T(8,128)(2,1)} %bitcast.12, bf16[128,8192]{1,0:T(8,128)(2,1)} %bitcast.13, bf16[128,1024]{1,0:T(8,128)(2,1)} %bitcast.16, bf16[128,4096]{1,0:T(8,128)(2,1)} %bitcast.14, ...), custom_call_target="tpu_custom_call" | custom-call | tf_op jit(solution)/shard_map/exchange/pallas_call | solution.py:463
  44.7 3.3 %head_product.1 = (bf16[4096,512]{1,0:T(8,128)(2,1)}, bf16[4096,256]{1,0:T(8,128)(2,1)}, bf16[512,256]{1,0:T(8,128)(2,1)}) custom-call(bf16[4096,256]{1,0:T(8,128)(2,1)S(1)} %get-tuple-element.7.head, bf16[256,512]{1,0:T(8,128)(2,1)S(1)} %bitcast.10, bf16[256,512]{1,0:T(8,128)(2,1)S(1)} %bitcast.11, bf16[512,256]{1,0:T(8,128)(2,1)S(1)} %get-tuple-element.10.head_own), custom_call_target="tpu_custom_call" | custom-call | tf_op jit(solution)/shard_map/head_product/pallas_call | solution.py:515

commit v3 on v2

--- a/solution.py
+++ b/solution.py
@@ -28,52 +28,50 @@
     return jnp.dot(a, b, preferred_element_type=F32)
 
 
+def each(first, last, body):
+    for k in range(first, last):
+        body(k, 0)
+
+
+def all_in(slots, count, sem):
+    some = slots.at[pl.ds(0, count)]
+    pltpu.make_async_copy(some, some, sem).wait()
+
+
 def iota(shape, dim):
     return lax.broadcasted_iota(jnp.int32, shape, dim)
 
 
 def exchange(
     acts, gq, gv, fa, fq, fv, own, task_of, layer_of, task_emb, layer_emb,
-    s_a, s_q, head, head_own,
+    s_a, s_q, head, head_own, prod_a,
     acts_v, gq_v, gv_v, fa_v, fq_v, fv_v, emb_v, own_v, task_v, layer_v,
     own_s, own_r, gat_a, gat_q, tr, a2, b2, v2,
     p_as, p_ar, p_qs, p_qr, z_as, z_ar, z_qs, z_qr, x_as, x_qs, big_a, big_q,
     load_sem, own_ss, own_rs, pa_ss, pa_rs, pq_ss, pq_rs, za_ss, za_rs, zq_ss, zq_rs, xa_ss, xa_rs, xq_ss, xq_rs,
 ):
     s, t = lax.axis_index("section"), lax.axis_index("tensor")
-    y, zh = s // 2, s % 2
-    zl, x, c = t // 8, (t // 2) % 4, t % 2
+    y, zh = lax.div(s, 2), lax.rem(s, 2)
+    zl, x, c = lax.div(t, 8), lax.rem(lax.div(t, 2), 4), lax.rem(t, 2)
     zdev = (zl * 2 + zh) * 2 + c
     xy = x * 4 + y
 
-    bar = pltpu.get_barrier_semaphore()
-
-    def greet(section, tensor):
-        pl.semaphore_signal(bar, inc=1, device_id=(section, tensor), device_id_type=MESH)
-
-    def greet_tensor(k, _):
-        greet(s, lax.rem(t + k, NT))
-        return 0
-
-    lax.fori_loop(1, NT, greet_tensor, 0)
-
-    def greet_z(k, _):
-        greet(y * 2 + 1 - zh, ((k // 2) * 4 + x) * 2 + k % 2)
-        return 0
-
-    lax.fori_loop(0, NZL * NC, greet_z, 0)
-
-    def greet_xy(k, _):
-        greet(lax.rem(y + 1 + k // 4, NY) * 2 + zh, (zl * 4 + k % 4) * 2 + c)
-        return 0
-
-    lax.fori_loop(0, (NY - 1) * NX, greet_xy, 0)
-
-    def greet_far(k, _):
-        greet(lax.rem(y + k, NY) * 2 + 1 - zh, t)
-        return 0
-
-    lax.fori_loop(1, NY, greet_far, 0)
+    def around(j, half):
+        return half + (j + 1) // 2 * (1 - 2 * (j % 2))
+
+    def tensor_peer(k):
+        return lax.rem(t + (k + 1), NT)
+
+    def z_peer(k):
+        z = lax.rem(zh * 4 + zl + around(k // 2, 4), 8)
+        to_c = lax.rem(c + 1 - (k % 2), 2)
+        to_zh = lax.div(z, 4)
+        to_zl = z - 4 * to_zh
+        return (to_zl * 2 + to_zh) * 2 + to_c, (y * 2 + to_zh, (to_zl * 4 + x) * 2 + to_c)
+
+    def xy_peer(k):
+        to_x, to_y = lax.rem(x + around(k // 4, 2), 4), lax.rem(y + around(k % 4, 2), 4)
+        return to_x * 4 + to_y, (to_y * 2 + zh, (zl * 4 + to_x) * 2 + c)
 
     loads = [
         pltpu.make_async_copy(src, dst, load_sem.at[i])
@@ -86,7 +84,39 @@
             )
         )
     ]
-    for load in loads:
+    for load in loads[:4]:
+        load.start()
+
+    bar = pltpu.get_barrier_semaphore()
+
+    def greet(section, tensor):
+        pl.semaphore_signal(bar, inc=1, device_id=(section, tensor), device_id_type=MESH)
+
+    def greet_tensor(k, _):
+        greet(s, tensor_peer(k))
+        return 0
+
+    each(0, NT - 1, greet_tensor)
+
+    def greet_z(k, _):
+        greet(y * 2 + 1 - zh, ((k // 2) * 4 + x) * 2 + (k % 2))
+        return 0
+
+    each(0, NZL * NC, greet_z)
+
+    def greet_xy(k, _):
+        greet(lax.rem(y + 1 + (k // 4), NY) * 2 + zh, (zl * 4 + (k % 4)) * 2 + c)
+        return 0
+
+    each(0, (NY - 1) * NX, greet_xy)
+
+    def greet_far(k, _):
+        greet(lax.rem(y + k, NY) * 2 + 1 - zh, t)
+        return 0
+
+    each(1, NY, greet_far)
+
+    for load in loads[4:]:
         load.start()
 
     loads[0].wait()
@@ -117,23 +147,16 @@
     pl.semaphore_wait(bar, (NT - 1) + NZL * NC + (NY - 1) * NX + NY - 1)
 
     def factor_copy(k, src, dst, send, recv):
-        to = lax.rem(t + k, NT)
+        to = tensor_peer(k)
         return pltpu.make_async_remote_copy(
-            src_ref=src.at[to], dst_ref=dst.at[t], send_sem=send.at[k], recv_sem=recv.at[t],
+            src_ref=src.at[to], dst_ref=dst.at[t], send_sem=send, recv_sem=recv,
             device_id=(s, to), device_id_type=MESH,
         )
-
-    def factor_arrived(k, dst, send, recv):
-        source = lax.rem(t + k, NT)
-        pltpu.make_async_remote_copy(
-            src_ref=dst.at[source], dst_ref=dst.at[source], send_sem=send.at[k], recv_sem=recv.at[source],
-            device_id=(s, source), device_id_type=MESH,
-        ).wait_recv()
 
     def own_copy(k):
         to = lax.rem(s + k, NS)
         return pltpu.make_async_remote_copy(
-            src_ref=own_s, dst_ref=own_r.at[s], send_sem=own_ss.at[k], recv_sem=own_rs.at[s],
+            src_ref=own_s, dst_ref=own_r.at[s], send_sem=own_ss, recv_sem=own_rs,
             device_id=(to, t), device_id_type=MESH,
         )
 
@@ -141,13 +164,13 @@
         own_copy(k).start()
         return 0
 
-    lax.fori_loop(1, NS, send_own, 0)
+    each(1, NS, send_own)
 
     def send_q(k, _):
         factor_copy(k, p_qs, p_qr, pq_ss, pq_rs).start()
         return 0
 
-    lax.fori_loop(1, NT, send_q, 0)
+    each(0, NT - 1, send_q)
 
     loads[3].wait()
     for i in range(16):
@@ -163,7 +186,7 @@
         factor_copy(k, p_as, p_ar, pa_ss, pa_rs).start()
         return 0
 
-    lax.fori_loop(1, NT, send_a, 0)
+    each(0, NT - 1, send_a)
 
     loads[4].wait()
 
@@ -221,11 +244,7 @@
 
     lax.fori_loop(0, 32, turn_a, 0, unroll=4)
 
-    def got_q(k, _):
-        factor_arrived(k, p_qr, pq_ss, pq_rs)
-        return 0
-
-    lax.fori_loop(1, NT, got_q, 0)
+    all_in(p_qr, NT - 1, pq_rs)
 
     places = [(zl_, zz, c_, x_) for zl_ in range(4) for zz in range(2) for c_ in range(2) for x_ in range(4)]
     backq = jnp.zeros((R, TOK), F32)
@@ -250,24 +269,13 @@
     lane = iota((TOK, 128), 1)
     diag = jnp.concatenate([jnp.where(lane // 16 == d, back, 0.0).astype(BF16) for d in range(8)], axis=0)
 
-    def z_peer(k):
-        q = lax.rem(zdev + k, 16)
-        return q, (y * 2 + (q // 2) % 2, ((q // 4) * 4 + x) * 2 + q % 2)
-
     def z_copy(k, src, dst, send, recv):
         q, device = z_peer(k)
         return pltpu.make_async_remote_copy(
-            src_ref=src.at[q], dst_ref=dst.at[zdev], send_sem=send.at[k], recv_sem=recv.at[zdev],
+            src_ref=src.at[q], dst_ref=dst.at[zdev], send_sem=send, recv_sem=recv,
             device_id=device, device_id_type=MESH,
         )
 
-    def z_arrived(k, dst, send, recv):
-        q, device = z_peer(k)
-        pltpu.make_async_remote_copy(
-            src_ref=dst.at[q], dst_ref=dst.at[q], send_sem=send.at[k], recv_sem=recv.at[q],
-            device_id=device, device_id_type=MESH,
-        ).wait_recv()
-
     for n in range(4):
         z_as[n * 4 : (n + 1) * 4] = (SCALE * mm(a2[n * 256 : (n + 1) * 256, :], diag)).astype(BF16).reshape(4, 64, 128)
 
@@ -275,18 +283,10 @@
         z_copy(k, z_as, z_ar, za_ss, za_rs).start()
         return 0
 
-    lax.fori_loop(1, 16, send_za, 0)
+    each(0, 15, send_za)
     z_ar[pl.ds(zdev, 1)] = z_as[pl.ds(zdev, 1)]
 
-    def got_own(k, _):
-        source = lax.rem(s + k, NS)
-        pltpu.make_async_remote_copy(
-            src_ref=own_s, dst_ref=own_r.at[source], send_sem=own_ss.at[k], recv_sem=own_rs.at[source],
-            device_id=(source, t), device_id_type=MESH,
-        ).wait_recv()
-        return 0
-
-    lax.fori_loop(1, NS, got_own, 0)
+    all_in(own_r, NS - 1, own_rs)
     for i in (7, 8, 9, 10):
         loads[i].wait()
     n_seq = NS * NT
@@ -315,11 +315,7 @@
 
     lax.fori_loop(0, HEAD_FIRST, head_block, 0)
 
-    def got_a(k, _):
-        factor_arrived(k, p_ar, pa_ss, pa_rs)
-        return 0
-
-    lax.fori_loop(1, NT, got_a, 0)
+    all_in(p_ar, NT - 1, pa_rs)
     fa_rows = jnp.concatenate([p_ar[(zl_ * 4 + x_) * 2 + c_, zz * 16 : (zz + 1) * 16, :] for zl_, zz, c_, x_ in places], axis=0)
     fa_t = fa_rows.astype(F32).T.astype(BF16)
     down_t = jnp.zeros((2 * R, TOK), F32)
@@ -342,7 +338,7 @@
         z_copy(k, z_qs, z_qr, zq_ss, zq_rs).start()
         return 0
 
-    lax.fori_loop(1, 16, send_zq, 0)
+    each(0, 15, send_zq)
     z_qr[pl.ds(zdev, 1)] = z_qs[pl.ds(zdev, 1)]
 
     lax.fori_loop(HEAD_FIRST, H // 256, head_block, 0)
@@ -350,24 +346,13 @@
     head_own[...] = head[pl.ds(pl.multiple_of(s * share, share), share), :]
 
     def xy_copy(k, src, dst, send, recv):
-        b = lax.rem(xy + k, 16)
+        b, device = xy_peer(k)
         return pltpu.make_async_remote_copy(
-            src_ref=src.at[b], dst_ref=dst.at[xy], send_sem=send.at[k], recv_sem=recv.at[xy],
-            device_id=((b % 4) * 2 + zh, (zl * 4 + b // 4) * 2 + c), device_id_type=MESH,
+            src_ref=src.at[b], dst_ref=dst.at[xy], send_sem=send, recv_sem=recv,
+            device_id=device, device_id_type=MESH,
         )
 
-    def xy_arrived(k, dst, send, recv):
-        b = lax.rem(xy + k, 16)
-        pltpu.make_async_remote_copy(
-            src_ref=dst.at[b], dst_ref=dst.at[b], send_sem=send.at[k], recv_sem=recv.at[b],
-            device_id=((b % 4) * 2 + zh, (zl * 4 + b // 4) * 2 + c), device_id_type=MESH,
-        ).wait_recv()
-
-    def got_za(k, _):
-        z_arrived(k, z_ar, za_ss, za_rs)
-        return 0
-
-    lax.fori_loop(1, 16, got_za, 0)
+    all_in(z_ar, 15, za_rs)
     big_a[...] = z_ar[...].astype(F32).reshape(1024, 128)
     for b in range(16):
         for i in range(4):
@@ -377,14 +362,10 @@
         xy_copy(k, x_as, s_a, xa_ss, xa_rs).start()
         return 0
 
-    lax.fori_loop(1, 16, send_xa, 0)
+    each(0, 15, send_xa)
     s_a[pl.ds(xy, 1)] = x_as[pl.ds(xy, 1)]
 
-    def got_zq(k, _):
-        z_arrived(k, z_qr, zq_ss, zq_rs)
-        return 0
-
-    lax.fori_loop(1, 16, got_zq, 0)
+    all_in(z_qr, 15, zq_rs)
     big_q[...] = z_qr[...].astype(F32).reshape(640, 128)
     for b in range(16):
         for i in range(2):
@@ -397,40 +378,33 @@
         xy_copy(k, x_qs, s_q, xq_ss, xq_rs).start()
         return 0
 
-    lax.fori_loop(1, 16, send_xq, 0)
+    each(0, 15, send_xq)
     s_q[pl.ds(xy, 1)] = x_qs[pl.ds(xy, 1)]
 
-    def sent_factors(k, _):
-        factor_copy(k, p_qs, p_qr, pq_ss, pq_rs).wait_send()
-        factor_copy(k, p_as, p_ar, pa_ss, pa_rs).wait_send()
-        return 0
-
-    lax.fori_loop(1, NT, sent_factors, 0)
-
-    def sent_own(k, _):
-        own_copy(k).wait_send()
-        return 0
-
-    lax.fori_loop(1, NS, sent_own, 0)
-
-    def sent_z(k, _):
-        z_copy(k, z_as, z_ar, za_ss, za_rs).wait_send()
-        z_copy(k, z_qs, z_qr, zq_ss, zq_rs).wait_send()
-        return 0
-
-    lax.fori_loop(1, 16, sent_z, 0)
-
-    def done_xy(k, _):
-        xy_arrived(k, s_a, xa_ss, xa_rs)
-        xy_arrived(k, s_q, xq_ss, xq_rs)
-        xy_copy(k, x_as, s_a, xa_ss, xa_rs).wait_send()
-        xy_copy(k, x_qs, s_q, xq_ss, xq_rs).wait_send()
-        return 0
-
-    lax.fori_loop(1, 16, done_xy, 0)
-
-
-def head_product(head, s_a, s_q, head_own, grad_a, grad_bq, grad_bv, a_v, q_v, v_v, sem):
+    all_in(s_a, 15, xa_rs)
+
+    def product(i, _):
+        at = pl.ds(pl.multiple_of(i * 512, 512), 512)
+        prod_a[at, :] = mm(head[at, :], s_a[...].reshape(256, 512)).astype(BF16)
+        return 0
+
+    lax.fori_loop(0, H // 512, product, 0)
+
+    all_in(p_qs, NT - 1, pq_ss)
+    all_in(p_as, NT - 1, pa_ss)
+
+    all_in(own_r, NS - 1, own_ss)
+
+    all_in(z_as, 15, za_ss)
+    all_in(z_qs, 15, zq_ss)
+
+    all_in(x_as, 15, xa_ss)
+    all_in(x_qs, 15, xq_ss)
+
+    all_in(s_q, 15, xq_rs)
+
+
+def head_product(head, prod_a, s_q, head_own, grad_a, grad_bq, grad_bv, q_v, v_v, sem):
     copies = []
 
     def write(src, dst, rows):
@@ -440,9 +414,8 @@
 
     step = H // PIECES
     for p in range(PIECES):
-        for r in range(p * step, (p + 1) * step, 256):
-            a_v[r : r + 256, :] = mm(head[r : r + 256, :], s_a[...]).astype(BF16)
-        write(a_v, grad_a, pl.ds(p * step, step))
+        write(prod_a, grad_a, pl.ds(p * step, step))
+    for p in range(PIECES):
         for r in range(p * step, (p + 1) * step, 256):
             q_v[r : r + 256, :] = mm(head[r : r + 256, :], s_q[:, 0:256]).astype(BF16)
         write(q_v, grad_bq, pl.ds(p * step, step))
@@ -460,16 +433,17 @@
         acts[0], grad_q[0], grad_v[0], fac_a[0], fac_bq[0], fac_bv[0], seq_tenant,
         tenant_task.reshape(1, TENANTS), section_layer.reshape(1, NS), task_emb, layer_emb,
     )
-    s_a, s_q, head, head_own = pl.pallas_call(
+    _, s_q, head, head_own, prod_a = pl.pallas_call(
         exchange,
         out_shape=(
             pltpu.VMEM((16, 16, 512), BF16),
             pltpu.VMEM((16, 16, 512), BF16),
             pltpu.VMEM((H, NS * NT), BF16),
             pltpu.VMEM((H // NS, NS * NT), BF16),
+            pltpu.VMEM((H, 512), BF16),
         ),
         in_specs=[hbm] * len(inputs),
-        out_specs=(vmem,) * 4,
+        out_specs=(vmem,) * 5,
         scratch_shapes=[
             pltpu.VMEM((TOK, 8192), BF16),
             pltpu.VMEM((TOK, 8192), BF16),
@@ -502,10 +476,7 @@
             pltpu.VMEM((1024, 128), F32),
             pltpu.VMEM((640, 128), F32),
             dma((len(inputs),)),
-            dma((NS,)), dma((NS,)),
-            dma((NT,)), dma((NT,)), dma((NT,)), dma((NT,)),
-            dma((16,)), dma((16,)), dma((16,)), dma((16,)),
-            dma((16,)), dma((16,)), dma((16,)), dma((16,)),
+            *([dma] * 14),
         ],
         compiler_params=pltpu.CompilerParams(
             collective_id=0, has_side_effects=True, vmem_limit_bytes=36 * 1024 * 1024
@@ -522,14 +493,13 @@
         in_specs=[vmem] * 4,
         out_specs=(hbm,) * 3,
         scratch_shapes=[
-            pltpu.VMEM((H, 512), BF16),
             pltpu.VMEM((H, 256), BF16),
             pltpu.VMEM((H // NS, 256), BF16),
             dma((2 * PIECES + 1,)),
         ],
         compiler_params=pltpu.CompilerParams(vmem_limit_bytes=20 * 1024 * 1024),
         name="head_product",
-    )(head, s_a.reshape(256, 512), s_q.reshape(256, 512), head_own)
+    )(head, prod_a, s_q.reshape(256, 512), head_own)
 
 
 def solution(mesh):

time: 48.1 us -> 45 us (0.936)
  Pallas kernels: 47.4 us -> 44.3 us
    pallas_call x1, Pallas kernels: 44.1 us -> 41.5 us  [shards(): pl.pallas_call(exchange, out_shape=(pltpu.VMEM((16, 16, 512), BF16), pltp...]
    pallas_call x1, Pallas kernels: 3.3 us -> 2.8 us  [shards(): pl.pallas_call(head_product, out_shape=(jax.ShapeDtypeStruct((H, 512), BF...]
where the time goes in v3:
time: 45 us; the launch traced here: 44.9 us
  Pallas kernels  44.3 us (98%)
  between operations  0.64 us (1%)
    pallas_call x1, Pallas kernels, shards(): pl.pallas_call(exchange, out_shape=(pltpu.VMEM((16, 16, 512), BF16), pltp...  41.5 us
    pallas_call x1, Pallas kernels, shards(): pl.pallas_call(head_product, out_shape=(jax.ShapeDtypeStruct((H, 512), BF...  2.8 us

profile of v3, /device:TPU:1, one launch (start us, length us, event | category | flops | bytes accessed | tf_op | source)
XLA Modules:
  0.0 44.9 jit_solution(10753977042748656021)
XLA Ops:
  0.6 41.5 %exchange.1 = (bf16[16,16,512]{2,1,0:T(8,128)(2,1)}, bf16[16,16,512]{2,1,0:T(8,128)(2,1)S(1)}, bf16[4096,256]{1,0:T(8,128)(2,1)S(1)}, bf16[512,256]{1,0:T(8,128)(2,1)S(1)}, bf16[4096,512]{1,0:T(8,128)(2,1)S(1)}) custom-call(bf16[128,8192]{1,0:T(8,128)(2,1)} %bitcast.10, bf16[128,8192]{1,0:T(8,128)(2,1)} %bitcast.11, bf16[128,1024]{1,0:T(8,128)(2,1)} %bitcast.14, ...), custom_call_target="tpu_custom_call" | custom-call | tf_op jit(solution)/shard_map/exchange/pallas_call | solution.py:436
  42.2 2.8 %head_product.1 = (bf16[4096,512]{1,0:T(8,128)(2,1)}, bf16[4096,256]{1,0:T(8,128)(2,1)}, bf16[512,256]{1,0:T(8,128)(2,1)}) custom-call(bf16[4096,256]{1,0:T(8,128)(2,1)S(1)} %get-tuple-element.7.head, bf16[4096,512]{1,0:T(8,128)(2,1)S(1)} %get-tuple-element.8.prod_a, bf16[256,512]{1,0:T(8,128)(2,1)S(1)} %bitcast.9, ...), custom_call_target="tpu_custom_call" | custom-call | tf_op jit(solution)/shard_map/head_product/pallas_call | solution.py:486

commit v4 on v3

--- a/solution.py
+++ b/solution.py
@@ -47,8 +47,8 @@
     s_a, s_q, head, head_own, prod_a,
     acts_v, gq_v, gv_v, fa_v, fq_v, fv_v, emb_v, own_v, task_v, layer_v,
     own_s, own_r, gat_a, gat_q, tr, a2, b2, v2,
-    p_as, p_ar, p_qs, p_qr, z_as, z_ar, z_qs, z_qr, x_as, x_qs, big_a, big_q,
-    load_sem, own_ss, own_rs, pa_ss, pa_rs, pq_ss, pq_rs, za_ss, za_rs, zq_ss, zq_rs, xa_ss, xa_rs, xq_ss, xq_rs,
+    p_as, p_ar, p_qs, p_qr, p_vs, p_vr, z_as, z_ar, z_qs, z_qr, x_as, x_qs, big_a, big_q,
+    load_sem, own_ss, own_rs, pa_ss, pa_rs, pq_ss, pq_rs, pv_ss, pv_rs, za_ss, za_rs, zq_ss, zq_rs, xa_ss, xa_rs, xq_ss, xq_rs,
 ):
     s, t = lax.axis_index("section"), lax.axis_index("tensor")
     y, zh = lax.div(s, 2), lax.rem(s, 2)
@@ -60,7 +60,7 @@
         return half + (j + 1) // 2 * (1 - 2 * (j % 2))
 
     def tensor_peer(k):
-        return lax.rem(t + (k + 1), NT)
+        return lax.rem(t + around(k, NT // 2), NT)
 
     def z_peer(k):
         z = lax.rem(zh * 4 + zl + around(k // 2, 4), 8)
@@ -92,29 +92,29 @@
     def greet(section, tensor):
         pl.semaphore_signal(bar, inc=1, device_id=(section, tensor), device_id_type=MESH)
 
+    def greet_z(k, _):
+        greet(y * 2 + 1 - zh, ((k // 2) * 4 + x) * 2 + (k % 2))
+        return 0
+
+    each(0, NZL * NC, greet_z)
+
+    def greet_xy(k, _):
+        greet(lax.rem(y + 1 + (k // 4), NY) * 2 + zh, (zl * 4 + (k % 4)) * 2 + c)
+        return 0
+
+    each(0, (NY - 1) * NX, greet_xy)
+
+    def greet_far(k, _):
+        greet(lax.rem(y + k, NY) * 2 + 1 - zh, t)
+        return 0
+
+    each(1, NY, greet_far)
+
     def greet_tensor(k, _):
         greet(s, tensor_peer(k))
         return 0
 
     each(0, NT - 1, greet_tensor)
-
-    def greet_z(k, _):
-        greet(y * 2 + 1 - zh, ((k // 2) * 4 + x) * 2 + (k % 2))
-        return 0
-
-    each(0, NZL * NC, greet_z)
-
-    def greet_xy(k, _):
-        greet(lax.rem(y + 1 + (k // 4), NY) * 2 + zh, (zl * 4 + (k % 4)) * 2 + c)
-        return 0
-
-    each(0, (NY - 1) * NX, greet_xy)
-
-    def greet_far(k, _):
-        greet(lax.rem(y + k, NY) * 2 + 1 - zh, t)
-        return 0
-
-    each(1, NY, greet_far)
 
     for load in loads[4:]:
         load.start()
@@ -132,17 +132,16 @@
         got = pick(fq_v[:, i * 256 : (i + 1) * 256])
         for h in range(2):
             yy, zz = i // 2, i % 2
-            gat_q[pl.ds(zz * 8 + yy * 2 + h, NT, stride=24), :] = got[:, h * 128 : (h + 1) * 128]
+            gat_q[pl.ds(zz * 8 + yy * 2 + h, NT, stride=16), :] = got[:, h * 128 : (h + 1) * 128]
     got = pick(fv_v[...])
     for h in range(2):
-        gat_q[pl.ds(16 + h, NT, stride=24), :] = got[:, h * 128 : (h + 1) * 128]
-    for h in range(6):
-        gat_q[pl.ds(18 + h, NT, stride=24), :] = jnp.zeros((NT, 128), F32)
-    p_qs[...] = gat_q[...].reshape(NT, 24, 128).astype(BF16)
+        p_vs[:, h, :] = got[:, h * 128 : (h + 1) * 128]
+    p_vr[pl.ds(t, 1)] = p_vs[pl.ds(t, 1)]
+    p_qs[...] = gat_q[...].reshape(NT, 16, 128).astype(BF16)
     p_qr[pl.ds(t, 1)] = p_qs[pl.ds(t, 1)]
 
-    own_s[...] = jnp.broadcast_to(jnp.concatenate([mine.astype(F32), jnp.zeros((1, 96), F32)], axis=1), (8, 128))
-    own_r[pl.ds(s, 1)] = own_s[...].reshape(1, 8, 128)
+    own_s[...] = jnp.concatenate([mine.astype(F32), jnp.zeros((1, 96), F32)], axis=1)
+    own_r[pl.ds(s, 1)] = own_s[...].reshape(1, 1, 128)
 
     pl.semaphore_wait(bar, (NT - 1) + NZL * NC + (NY - 1) * NX + NY - 1)
 
@@ -164,13 +163,14 @@
         own_copy(k).start()
         return 0
 
+
+    def send_q(k, _):
+        factor_copy(k, p_vs, p_vr, pv_ss, pv_rs).start()
+        factor_copy(k, p_qs, p_qr, pq_ss, pq_rs).start()
+        return 0
+
+    each(0, NT - 1, send_q)
     each(1, NS, send_own)
-
-    def send_q(k, _):
-        factor_copy(k, p_qs, p_qr, pq_ss, pq_rs).start()
-        return 0
-
-    each(0, NT - 1, send_q)
 
     loads[3].wait()
     for i in range(16):
@@ -244,6 +244,7 @@
 
     lax.fori_loop(0, 32, turn_a, 0, unroll=4)
 
+    all_in(p_vr, NT - 1, pv_rs)
     all_in(p_qr, NT - 1, pq_rs)
 
     places = [(zl_, zz, c_, x_) for zl_ in range(4) for zz in range(2) for c_ in range(2) for x_ in range(4)]
@@ -256,7 +257,7 @@
         part = mm(fq_t[n * 16 : (n + 1) * 16], b2[:, n * 256 : (n + 1) * 256])
         backq = backq + part[0:8, 0:128] + part[8:16, 128:256]
     fv_rows = jnp.concatenate(
-        [p_qr[(zl_ * 4 + x_) * 2 + c_, 16:24, :].astype(F32)[0:2] for zl_ in range(4) for c_ in range(2) for x_ in range(4)],
+        [p_vr[(zl_ * 4 + x_) * 2 + c_] for zl_ in range(4) for c_ in range(2) for x_ in range(4)],
         axis=0,
     )
     fv_t = jnp.concatenate([fv_rows, jnp.zeros((64, 128), F32)], axis=0).T.astype(BF16)[:, 0:64]
@@ -293,7 +294,7 @@
     col = iota((1, n_seq), 1)
     col_s = (col // 16 % 4) * 2 + (col // 2) % 2
     col_t = ((col // 4 % 4) * 4 + col // 64) * 2 + col % 2
-    owners = jnp.concatenate([own_r[i, 0:1, :] for i in range(NS)], axis=0)
+    owners = jnp.concatenate([own_r[i] for i in range(NS)], axis=0)
     spread = mm(owners.astype(BF16), (iota((128, n_seq), 0) == col_t).astype(F32).astype(BF16))
     in_section = iota((NS, n_seq), 0) == col_s
     tenant = jnp.sum(jnp.where(in_section, spread, 0.0), axis=0, keepdims=True)
@@ -390,6 +391,7 @@
 
     lax.fori_loop(0, H // 512, product, 0)
 
+    all_in(p_vs, NT - 1, pv_ss)
     all_in(p_qs, NT - 1, pq_ss)
     all_in(p_as, NT - 1, pa_ss)
 
@@ -455,18 +457,20 @@
             pltpu.VMEM((1, NT), jnp.int32),
             pltpu.VMEM((1, TENANTS), jnp.int32),
             pltpu.VMEM((1, NS), jnp.int32),
-            pltpu.VMEM((8, 128), F32),
-            pltpu.VMEM((NS, 8, 128), F32),
+            pltpu.VMEM((1, 128), F32),
+            pltpu.VMEM((NS, 1, 128), F32),
             pltpu.VMEM((NT * 32, 128), F32),
-            pltpu.VMEM((NT * 24, 128), F32),
+            pltpu.VMEM((NT * 16, 128), F32),
             pltpu.VMEM((1024, 128), F32),
             pltpu.VMEM((1024, 1024), BF16),
             pltpu.VMEM((512, 2048), BF16),
             pltpu.VMEM((64, 2048), BF16),
             pltpu.VMEM((NT, 32, 128), BF16),
             pltpu.VMEM((NT, 32, 128), BF16),
-            pltpu.VMEM((NT, 24, 128), BF16),
-            pltpu.VMEM((NT, 24, 128), BF16),
+            pltpu.VMEM((NT, 16, 128), BF16),
+            pltpu.VMEM((NT, 16, 128), BF16),
+            pltpu.VMEM((NT, 2, 128), F32),
+            pltpu.VMEM((NT, 2, 128), F32),
             pltpu.VMEM((16, 64, 128), BF16),
             pltpu.VMEM((16, 64, 128), BF16),
             pltpu.VMEM((16, 40, 128), BF16),
@@ -476,7 +480,7 @@
             pltpu.VMEM((1024, 128), F32),
             pltpu.VMEM((640, 128), F32),
             dma((len(inputs),)),
-            *([dma] * 14),
+            *([dma] * 16),
         ],
         compiler_params=pltpu.CompilerParams(
             collective_id=0, has_side_effects=True, vmem_limit_bytes=36 * 1024 * 1024

time: 45 us -> 42.2 us (0.938)
  Pallas kernels: 44.3 us -> 41.4 us
    pallas_call x1, Pallas kernels: 41.5 us -> 38.6 us  [shards(): pl.pallas_call(exchange, out_shape=(pltpu.VMEM((16, 16, 512), BF16), pltp...]
where the time goes in v4:
time: 42.2 us; the launch traced here: 42.1 us
  Pallas kernels  41.4 us (98%)
  between operations  0.64 us (2%)
    pallas_call x1, Pallas kernels, shards(): pl.pallas_call(exchange, out_shape=(pltpu.VMEM((16, 16, 512), BF16), pltp...  38.6 us
    pallas_call x1, Pallas kernels, shards(): pl.pallas_call(head_product, out_shape=(jax.ShapeDtypeStruct((H, 512), BF...  2.8 us

profile of v4, /device:TPU:1, one launch (start us, length us, event | category | flops | bytes accessed | tf_op | source)
XLA Modules:
  0.0 42.1 jit_solution(962249738620408945)
XLA Ops:
  0.6 38.6 %exchange.1 = (bf16[16,16,512]{2,1,0:T(8,128)(2,1)}, bf16[16,16,512]{2,1,0:T(8,128)(2,1)S(1)}, bf16[4096,256]{1,0:T(8,128)(2,1)S(1)}, bf16[512,256]{1,0:T(8,128)(2,1)S(1)}, bf16[4096,512]{1,0:T(8,128)(2,1)S(1)}) custom-call(bf16[128,8192]{1,0:T(8,128)(2,1)} %bitcast.10, bf16[128,8192]{1,0:T(8,128)(2,1)} %bitcast.11, bf16[128,1024]{1,0:T(8,128)(2,1)} %bitcast.14, ...), custom_call_target="tpu_custom_call" | custom-call | tf_op jit(solution)/shard_map/exchange/pallas_call | solution.py:438
  39.3 2.8 %head_product.1 = (bf16[4096,512]{1,0:T(8,128)(2,1)}, bf16[4096,256]{1,0:T(8,128)(2,1)}, bf16[512,256]{1,0:T(8,128)(2,1)}) custom-call(bf16[4096,256]{1,0:T(8,128)(2,1)S(1)} %get-tuple-element.7.head, bf16[4096,512]{1,0:T(8,128)(2,1)S(1)} %get-tuple-element.8.prod_a, bf16[256,512]{1,0:T(8,128)(2,1)S(1)} %bitcast.9, ...), custom_call_target="tpu_custom_call" | custom-call | tf_op jit(solution)/shard_map/head_product/pallas_call | solution.py:490

commit v5 on v4

--- a/solution.py
+++ b/solution.py
@@ -63,8 +63,8 @@
         return lax.rem(t + around(k, NT // 2), NT)
 
     def z_peer(k):
-        z = lax.rem(zh * 4 + zl + around(k // 2, 4), 8)
-        to_c = lax.rem(c + 1 - (k % 2), 2)
+        z = lax.rem(zh * 4 + zl + around(k % 8, 4), 8)
+        to_c = lax.rem(c + 1 - k // 8, 2)
         to_zh = lax.div(z, 4)
         to_zl = z - 4 * to_zh
         return (to_zl * 2 + to_zh) * 2 + to_c, (y * 2 + to_zh, (to_zl * 4 + x) * 2 + to_c)
@@ -170,7 +170,6 @@
         return 0
 
     each(0, NT - 1, send_q)
-    each(1, NS, send_own)
 
     loads[3].wait()
     for i in range(16):
@@ -187,6 +186,7 @@
         return 0
 
     each(0, NT - 1, send_a)
+    each(1, NS, send_own)
 
     loads[4].wait()
 
@@ -329,11 +329,11 @@
     diag_q = jnp.concatenate([jnp.where(lane // 8 == e, down_q, 0.0).astype(BF16) for e in range(16)], axis=0)
     diag_v = jnp.concatenate([jnp.where(lane // 8 == e, down_v, 0.0).astype(BF16) for e in range(16)], axis=0)
     grad_v_rows = SCALE * mm(v2[...], diag_v)
-    grad_v_rows = grad_v_rows.reshape(8, 8, 128).astype(BF16)
+    grad_v_rows = jnp.concatenate([grad_v_rows.reshape(8, 8, 128), jnp.zeros((8, 8, 128), F32)], axis=1).astype(BF16)
     grad_q_rows = (SCALE * mm(b2[...], diag_q)).astype(BF16).reshape(16, 32, 128)
     for q in range(16):
         z_qs[q, 0:32, :] = grad_q_rows[q]
-        z_qs[q, 32:40, :] = grad_v_rows[(q // 4) * 2 + q % 2]
+        z_qs[q, 32:48, :] = grad_v_rows[(q // 4) * 2 + q % 2]
 
     def send_zq(k, _):
         z_copy(k, z_qs, z_qr, zq_ss, zq_rs).start()
@@ -367,12 +367,12 @@
     s_a[pl.ds(xy, 1)] = x_as[pl.ds(xy, 1)]
 
     all_in(z_qr, 15, zq_rs)
-    big_q[...] = z_qr[...].astype(F32).reshape(640, 128)
+    big_q[...] = z_qr[...].astype(F32).reshape(768, 128)
     for b in range(16):
         for i in range(2):
-            x_qs[b, :, i * 128 : (i + 1) * 128] = big_q[pl.ds(b * 2 + i, 16, stride=40), :].astype(BF16)
+            x_qs[b, :, i * 128 : (i + 1) * 128] = big_q[pl.ds(b * 2 + i, 16, stride=48), :].astype(BF16)
             x_qs[b, :, 256 + i * 128 : 256 + (i + 1) * 128] = big_q[
-                pl.ds(32 + (b // 4) * 2 + i, 16, stride=40), :
+                pl.ds(32 + (b // 4) * 2 + i, 16, stride=48), :
             ].astype(BF16)
 
     def send_xq(k, _):
@@ -473,12 +473,12 @@
             pltpu.VMEM((NT, 2, 128), F32),
             pltpu.VMEM((16, 64, 128), BF16),
             pltpu.VMEM((16, 64, 128), BF16),
-            pltpu.VMEM((16, 40, 128), BF16),
-            pltpu.VMEM((16, 40, 128), BF16),
+            pltpu.VMEM((16, 48, 128), BF16),
+            pltpu.VMEM((16, 48, 128), BF16),
             pltpu.VMEM((16, 16, 512), BF16),
             pltpu.VMEM((16, 16, 512), BF16),
             pltpu.VMEM((1024, 128), F32),
-            pltpu.VMEM((640, 128), F32),
+            pltpu.VMEM((768, 128), F32),
             dma((len(inputs),)),
             *([dma] * 16),
         ],

time: 42.2 us -> 42.8 us (1.014)
  Pallas kernels: 41.4 us -> 42 us
    pallas_call x1, Pallas kernels: 38.6 us -> 39.2 us  [shards(): pl.pallas_call(exchange, out_shape=(pltpu.VMEM((16, 16, 512), BF16), pltp...]
where the time goes in v5:
time: 42.8 us; the launch traced here: 42.7 us
  Pallas kernels  42 us (98%)
  between operations  0.64 us (1%)
    pallas_call x1, Pallas kernels, shards(): pl.pallas_call(exchange, out_shape=(pltpu.VMEM((16, 16, 512), BF16), pltp...  39.2 us
    pallas_call x1, Pallas kernels, shards(): pl.pallas_call(head_product, out_shape=(jax.ShapeDtypeStruct((H, 512), BF...  2.8 us

profile of v5, /device:TPU:1, one launch (start us, length us, event | category | flops | bytes accessed | tf_op | source)
XLA Modules:
  0.0 42.7 jit_solution(8322906067635518895)
XLA Ops:
  0.6 39.2 %exchange.1 = (bf16[16,16,512]{2,1,0:T(8,128)(2,1)}, bf16[16,16,512]{2,1,0:T(8,128)(2,1)S(1)}, bf16[4096,256]{1,0:T(8,128)(2,1)S(1)}, bf16[512,256]{1,0:T(8,128)(2,1)S(1)}, bf16[4096,512]{1,0:T(8,128)(2,1)S(1)}) custom-call(bf16[128,8192]{1,0:T(8,128)(2,1)} %bitcast.10, bf16[128,8192]{1,0:T(8,128)(2,1)} %bitcast.11, bf16[128,1024]{1,0:T(8,128)(2,1)} %bitcast.14, ...), custom_call_target="tpu_custom_call" | custom-call | tf_op jit(solution)/shard_map/exchange/pallas_call | solution.py:438
  39.9 2.8 %head_product.1 = (bf16[4096,512]{1,0:T(8,128)(2,1)}, bf16[4096,256]{1,0:T(8,128)(2,1)}, bf16[512,256]{1,0:T(8,128)(2,1)}) custom-call(bf16[4096,256]{1,0:T(8,128)(2,1)S(1)} %get-tuple-element.7.head, bf16[4096,512]{1,0:T(8,128)(2,1)S(1)} %get-tuple-element.8.prod_a, bf16[256,512]{1,0:T(8,128)(2,1)S(1)} %bitcast.9, ...), custom_call_target="tpu_custom_call" | custom-call | tf_op jit(solution)/shard_map/head_product/pallas_call | solution.py:490

commit v6 on v5

--- a/solution.py
+++ b/solution.py
@@ -19,7 +19,7 @@
 TOK = 128
 NS, NT = 8, 32
 NX, NY, NZL, NZH, NC = 4, 4, 4, 2, 2
-HEAD_FIRST = 8
+HEAD_FIRST = 10
 PIECES = 4
 SCALE = 2.0 / math.sqrt(TOK * NT * NS)
 
@@ -63,8 +63,8 @@
         return lax.rem(t + around(k, NT // 2), NT)
 
     def z_peer(k):
-        z = lax.rem(zh * 4 + zl + around(k % 8, 4), 8)
-        to_c = lax.rem(c + 1 - k // 8, 2)
+        z = lax.rem(zh * 4 + zl + around(k // 2, 4), 8)
+        to_c = lax.rem(c + 1 - (k % 2), 2)
         to_zh = lax.div(z, 4)
         to_zl = z - 4 * to_zh
         return (to_zl * 2 + to_zh) * 2 + to_c, (y * 2 + to_zh, (to_zl * 4 + x) * 2 + to_c)

time: 42.8 us -> 42.8 us (level)
  no operation moved by 1% of the time
where the time goes in v6:
time: 42.8 us; the launch traced here: 42.7 us
  Pallas kernels  42.1 us (98%)
  between operations  0.64 us (1%)
    pallas_call x1, Pallas kernels, shards(): pl.pallas_call(exchange, out_shape=(pltpu.VMEM((16, 16, 512), BF16), pltp...  39.3 us
    pallas_call x1, Pallas kernels, shards(): pl.pallas_call(head_product, out_shape=(jax.ShapeDtypeStruct((H, 512), BF...  2.8 us

profile of v6, /device:TPU:1, one launch (start us, length us, event | category | flops | bytes accessed | tf_op | source)
XLA Modules:
  0.0 42.7 jit_solution(10792641150098700593)
XLA Ops:
  0.6 39.3 %exchange.1 = (bf16[16,16,512]{2,1,0:T(8,128)(2,1)}, bf16[16,16,512]{2,1,0:T(8,128)(2,1)S(1)}, bf16[4096,256]{1,0:T(8,128)(2,1)S(1)}, bf16[512,256]{1,0:T(8,128)(2,1)S(1)}, bf16[4096,512]{1,0:T(8,128)(2,1)S(1)}) custom-call(bf16[128,8192]{1,0:T(8,128)(2,1)} %bitcast.10, bf16[128,8192]{1,0:T(8,128)(2,1)} %bitcast.11, bf16[128,1024]{1,0:T(8,128)(2,1)} %bitcast.14, ...), custom_call_target="tpu_custom_call" | custom-call | tf_op jit(solution)/shard_map/exchange/pallas_call | solution.py:438
  39.9 2.8 %head_product.1 = (bf16[4096,512]{1,0:T(8,128)(2,1)}, bf16[4096,256]{1,0:T(8,128)(2,1)}, bf16[512,256]{1,0:T(8,128)(2,1)}) custom-call(bf16[4096,256]{1,0:T(8,128)(2,1)S(1)} %get-tuple-element.7.head, bf16[4096,512]{1,0:T(8,128)(2,1)S(1)} %get-tuple-element.8.prod_a, bf16[256,512]{1,0:T(8,128)(2,1)S(1)} %bitcast.9, ...), custom_call_target="tpu_custom_call" | custom-call | tf_op jit(solution)/shard_map/head_product/pallas_call | solution.py:490
